TPU v7x, 512 devices: a whole 4x8x8 slice. The times are simulated.
512 devices in a mesh: seq: 128 (over z, y, core), spill: 4 (over x).
Axes of the slice: x: 4, y: 8, z: 8, core: 2. Of those that a mesh axis runs over, the one named last changes fastest.
Arguments:
- queries: bfloat16 [65536, 1024], P(('seq', 'spill')), may hold values from -192 to 192
- keys: bfloat16 [65536, 1024], P(('seq', 'spill')), may hold values from -6 to 6
- values: bfloat16 [65536, 1024], P(('seq', 'spill')), may hold values from -6 to 6
- out_grad: bfloat16 [65536, 1024], P(('seq', 'spill')), may hold values from -6 to 6
- cluster_ids: int32 [65536, 8], P(('seq', 'spill')), may hold values from 0 to 255, as said below
Outputs:
- query_grad: bfloat16 [65536, 1024], P(('seq', 'spill'))
- key_grad: bfloat16 [65536, 1024], P(('seq', 'spill'))
- value_grad: bfloat16 [65536, 1024], P(('seq', 'spill'))
Inputs may be any that keep to these rules, and one draw needn't show every extreme that they name: `cluster_ids`: cluster c belongs to owner c % 128. In every aligned block of 128 rows and every head, at most 2 rows name clusters of one owner; in every draw some block reaches 2 for some owner, and in one head every block sends 2 rows to one common owner.
All inputs are finite; a program needn't handle non-finite values.
Results may differ from a plain program's by a relative error of at most 0.012.
Values may be sent and summed in bfloat16 or wider, within the bound.
No kernel may reach another device: no remote copies, remote signals or barrier semaphores. Data moves between devices by JAX's collectives and lax.ppermute only.
A program may use at most 64 MiB of HBM per device.

v0:
```python
import jax
import jax.numpy as jnp
from jax import lax
from jax.sharding import PartitionSpec as P

CLU_DEV = 2


MASKED_SCORE = -1e30


def for_sending(value):
    return jax.tree.map(lambda a: a.astype(jnp.bfloat16) if a.dtype == jnp.float32 else a, value)


def contract_last(left, right):
    return lax.dot_general(
        left, right, (((1,), (1,)), ((), ())), preferred_element_type=jnp.float32
    )


def contract_first(left, right):
    return lax.dot_general(
        left, right, (((0,), (0,)), ((), ())), preferred_element_type=jnp.float32
    )


def softmax_parts(q_rows, g_rows, q_label, k_rows, v_rows, k_label, per_owner):
    score_scale = q_rows.shape[1] ** (-0.5)
    raw_scores = contract_last(q_rows, k_rows) * score_scale
    live_pair = (q_label[:, None] >= 0) & (k_label[None, :] >= 0)
    same_cluster = q_label[:, None] % per_owner == k_label[None, :] % per_owner
    causal_pair = k_label[None, :] // per_owner <= q_label[:, None] // per_owner
    allowed = live_pair & same_cluster & causal_pair
    row_max = jnp.max(jnp.where(allowed, raw_scores, MASKED_SCORE), axis=1, keepdims=True)
    weights_raw = jnp.where(allowed, jnp.exp(raw_scores - row_max), 0.0)
    row_total = jnp.maximum(jnp.sum(weights_raw, axis=1, keepdims=True), 1.0)
    probability = weights_raw / row_total
    prob_half = probability.astype(jnp.bfloat16)
    attended = jnp.dot(prob_half, v_rows, preferred_element_type=jnp.float32)
    row_delta = jnp.sum(g_rows.astype(jnp.float32) * attended, axis=1, keepdims=True)
    prob_grad = contract_last(g_rows, v_rows)
    score_grad = (probability * (prob_grad - row_delta) * score_scale).astype(jnp.bfloat16)
    return (prob_half, score_grad)


def local(queries, keys, values, out_grad, cluster_ids):
    tok_rows, row_width = queries.shape
    head_count = cluster_ids.shape[1]
    head_size = row_width // head_count
    seq_count = lax.axis_size("seq")
    spill_count = lax.axis_size("spill")
    capacity = max(1, 2 * tok_rows // seq_count)
    slot_count = seq_count * capacity
    per_owner = CLU_DEV
    device_index = lax.axis_index("seq") * spill_count + lax.axis_index("spill")
    position = device_index * tok_rows + jnp.arange(tok_rows, dtype=jnp.int32)
    ids_by_head = jnp.transpose(cluster_ids)
    owner_of = ids_by_head % seq_count
    local_cluster = ids_by_head // seq_count
    same_owner = owner_of[:, :, None] == owner_of[:, None, :]
    token_iota = jnp.arange(tok_rows, dtype=jnp.int32)
    earlier = token_iota[None, :] < token_iota[:, None]
    rank_in = jnp.sum((same_owner & earlier[None]).astype(jnp.int32), axis=2)
    slot_of = owner_of * capacity + rank_in
    dispatch = slot_of[:, None, :] == jnp.arange(slot_count, dtype=jnp.int32)[None, :, None]
    dispatch_half = dispatch.astype(jnp.bfloat16)
    token_label = position[None, :] * per_owner + local_cluster
    slot_label = jnp.sum(jnp.where(dispatch, token_label[:, None, :] + 1, 0), axis=2) - 1

    def place(matrix):
        per_head = matrix.reshape(tok_rows, head_count, head_size)
        placed = jnp.einsum(
            "hst,thd->hsd", dispatch_half, per_head, preferred_element_type=jnp.float32
        )
        return placed.astype(jnp.bfloat16).reshape(head_count, seq_count, capacity, head_size)

    routed = (
        lax.all_to_all(place(queries), "seq", split_axis=1, concat_axis=1, tiled=True),
        lax.all_to_all(place(keys), "seq", split_axis=1, concat_axis=1, tiled=True),
        lax.all_to_all(place(values), "seq", split_axis=1, concat_axis=1, tiled=True),
        lax.all_to_all(place(out_grad), "seq", split_axis=1, concat_axis=1, tiled=True),
        lax.all_to_all(
            slot_label.reshape(head_count, seq_count, capacity),
            "seq",
            split_axis=1,
            concat_axis=1,
            tiled=True,
        ),
    )
    q_slots = routed[0].reshape(head_count, slot_count, head_size)
    k_slots = routed[1].reshape(head_count, slot_count, head_size)
    v_slots = routed[2].reshape(head_count, slot_count, head_size)
    g_slots = routed[3].reshape(head_count, slot_count, head_size)
    label_slots = routed[4].reshape(head_count, slot_count)
    k_group, v_group, label_group = (
        lax.all_gather(k_slots, "spill", axis=1, tiled=True),
        lax.all_gather(v_slots, "spill", axis=1, tiled=True),
        lax.all_gather(for_sending(label_slots), "spill", axis=1, tiled=True).astype(
            label_slots.dtype
        ),
    )

    def per_head_keys(per_item):
        q_rows, g_rows, q_label, k_rows, v_rows, k_label = per_item
        prob_half, score_grad = softmax_parts(
            q_rows, g_rows, q_label, k_rows, v_rows, k_label, per_owner
        )
        query_part = jnp.dot(score_grad, k_rows, preferred_element_type=jnp.float32).astype(
            jnp.bfloat16
        )
        return (query_part, contract_first(score_grad, q_rows), contract_first(prob_half, g_rows))

    query_slots, key_terms, value_terms = lax.map(
        per_head_keys, (q_slots, g_slots, label_slots, k_group, v_group, label_group)
    )
    key_sum, value_sum = (
        lax.psum_scatter(
            key_terms.astype(jnp.bfloat16), "spill", scatter_dimension=1, tiled=True
        ).astype(jnp.float32),
        lax.psum_scatter(
            value_terms.astype(jnp.bfloat16), "spill", scatter_dimension=1, tiled=True
        ).astype(jnp.float32),
    )
    key_slots = key_sum.astype(jnp.bfloat16)
    value_slots = value_sum.astype(jnp.bfloat16)
    shaped = (head_count, seq_count, capacity, head_size)
    returned = (
        lax.all_to_all(query_slots.reshape(shaped), "seq", split_axis=1, concat_axis=1, tiled=True),
        lax.all_to_all(key_slots.reshape(shaped), "seq", split_axis=1, concat_axis=1, tiled=True),
        lax.all_to_all(value_slots.reshape(shaped), "seq", split_axis=1, concat_axis=1, tiled=True),
    )

    def unplace(buffer):
        rows_back = jnp.einsum(
            "hst,hsd->thd",
            dispatch_half,
            buffer.reshape(head_count, slot_count, head_size),
            preferred_element_type=jnp.float32,
        )
        return rows_back.astype(jnp.bfloat16).reshape(tok_rows, row_width)

    return (unplace(returned[0]), unplace(returned[1]), unplace(returned[2]))


def solution(mesh):
    placed = (
        P(("seq", "spill"), None),
        P(("seq", "spill"), None),
        P(("seq", "spill"), None),
        P(("seq", "spill"), None),
        P(("seq", "spill"), None),
    )
    return jax.shard_map(
        local,
        mesh=mesh,
        in_specs=placed,
        out_specs=(P(("seq", "spill"), None), P(("seq", "spill"), None), P(("seq", "spill"), None)),
        check_vma=False,
    )
```

profile of v0, /device:TPU:1, one launch (start us, length us, event | category | flops | bytes accessed | tf_op | source)
XLA Modules:
  0.0 325.4 jit_solution(7848126205741023390)
XLA Ops:
  9.7 38.8 %all_to_all.40 = bf16[8,128,2,128]{3,2,0,1:T(2,128)(2,1)S(1)} all-to-all(bf16[8,128,2,128]{3,2,0,1:T(2,128)(2,1)S(1)} %copy.121), channel_id=1, replica_groups=mesh['seq'=128,'spill'=4] {'seq'}, dimensions={1} | all-to-all | bytes 1048576 | tf_op jit(solution)/shard_map/all_to_all | solution.py:81
  50.2 25.8 %all_to_all.41 = bf16[8,128,2,128]{3,2,0,1:T(2,128)(2,1)S(1)} all-to-all(bf16[8,128,2,128]{3,2,0,1:T(2,128)(2,1)S(1)} %copy.116), channel_id=1, replica_groups=mesh['seq'=128,'spill'=4] {'seq'}, dimensions={1} | all-to-all | bytes 1048576 | tf_op jit(solution)/shard_map/all_to_all | solution.py:80
  78.2 5.4 %all-to-all-start = ((s32[8,128,2]{0,2,1:T(2,128)}), s32[8,128,2]{0,2,1:T(2,128)S(1)}, u32[]{:S(2)}, u32[]{:S(2)}) async-start(s32[8,128,2]{0,2,1:T(2,128)} %bitcast.11), calls=%async_computation | async-start | bytes 262144 | tf_op jit(solution)/shard_map/all_to_all | solution.py:83
  83.9 1.4 copy.119
  85.3 11.0 %all-to-all-done = s32[8,128,2]{0,2,1:T(2,128)S(1)} async-done(((s32[8,128,2]{0,2,1:T(2,128)}), s32[8,128,2]{0,2,1:T(2,128)S(1)}, u32[]{:S(2)}, u32[]{:S(2)}) %all-to-all-start) | async-done | bytes 8224 | tf_op jit(solution)/shard_map/all_to_all | solution.py:83
  96.3 5.6 %all-to-all-start.3 = ((bf16[8,128,2,128]{3,0,2,1:T(8,128)(2,1)}), bf16[8,128,2,128]{3,0,2,1:T(8,128)(2,1)S(1)}, u32[]{:S(2)}, u32[]{:S(2)}) async-start(bf16[8,128,2,128]{3,0,2,1:T(8,128)(2,1)} %copy.119), calls=%async_computation.3 | async-start | bytes 1048576 | tf_op jit(solution)/shard_map/all_to_all | solution.py:82
  102.2 1.2 copy.113
  103.4 19.2 %all-to-all-done.3 = bf16[8,128,2,128]{3,0,2,1:T(8,128)(2,1)S(1)} async-done(((bf16[8,128,2,128]{3,0,2,1:T(8,128)(2,1)}), bf16[8,128,2,128]{3,0,2,1:T(8,128)(2,1)S(1)}, u32[]{:S(2)}, u32[]{:S(2)}) %all-to-all-start.3) | async-done | bytes 524320 | tf_op jit(solution)/shard_map/all_to_all | solution.py:82
  122.6 5.4 %all-to-all-start.1 = ((bf16[8,128,2,128]{3,2,0,1:T(2,128)(2,1)}), bf16[8,128,2,128]{3,2,0,1:T(2,128)(2,1)S(1)}, u32[]{:S(2)}, u32[]{:S(2)}) async-start(bf16[8,128,2,128]{3,2,0,1:T(2,128)(2,1)} %copy.113), calls=%async_computation.1 | async-start | bytes 1048576 | tf_op jit(solution)/shard_map/all_to_all | solution.py:79
  128.1 11.8 %all_gather.9 = s32[8,1024]{0,1:T(8,128)S(1)} all-gather(s32[8,256]{0,1:T(8,128)S(1)} %bitcast.162), channel_id=1, replica_groups=mesh['seq'=128,'spill'=4] {'spill'}, dimensions={1}, use_global_device_ids=true | all-gather | bytes 40960 | tf_op jit(solution)/shard_map/all_gather | solution.py:99
  140.4 8.1 %all-to-all-done.1 = bf16[8,128,2,128]{3,2,0,1:T(2,128)(2,1)S(1)} async-done(((bf16[8,128,2,128]{3,2,0,1:T(2,128)(2,1)}), bf16[8,128,2,128]{3,2,0,1:T(2,128)(2,1)S(1)}, u32[]{:S(2)}, u32[]{:S(2)}) %all-to-all-start.1) | async-done | bytes 524320 | tf_op jit(solution)/shard_map/all_to_all | solution.py:79
  148.8 1.9 copy.128
  150.7 3.2 copy.126
  153.9 60.1 %while.17 = (s32[]{:T(128)}, bf16[8,256,128]{2,1,0:T(8,128)(2,1)}, bf16[8,1024,128]{2,1,0:T(8,128)(2,1)}, bf16[8,1024,128]{2,1,0:T(8,128)(2,1)}, s32[8,256]{1,0:...) while((s32[]{:T(128)}, bf16[8,256,128]{2,1,0:T(8,128)(2,1)}, ...), condition=%wide.region_6.7_spmd, body=%wide.region_2.6_spmd.sunk | while | flops 410677760 | bytes 11489669 | solution.py:114
  154.0 1.5 select_reduce_fusion.3
  157.4 1.9 fusion.94
  159.3 1.1 fusion.96
  161.5 1.5 select_reduce_fusion.3
  164.9 1.9 fusion.94
  166.8 1.1 fusion.96
  167.8 1.1 fusion.95
  169.0 1.5 select_reduce_fusion.3
  172.4 1.9 fusion.94
  175.3 1.1 fusion.95
  176.5 1.5 select_reduce_fusion.3
  179.9 1.9 fusion.94
  184.0 1.5 select_reduce_fusion.3
  187.4 1.9 fusion.94
  190.3 1.1 fusion.95
  191.5 1.5 select_reduce_fusion.3
  194.9 1.9 fusion.94
  196.8 1.1 fusion.96
  197.8 1.1 fusion.95
  199.0 1.5 select_reduce_fusion.3
  202.4 1.9 fusion.94
  205.3 1.1 fusion.95
  206.5 1.5 select_reduce_fusion.3
  209.9 1.9 fusion.94
  211.8 1.1 fusion.96
  215.0 1.1 copy.129
  216.1 6.9 %all-to-all-start.5 = ((bf16[8,128,2,128]{3,0,2,1:T(8,128)(2,1)}), bf16[8,128,2,128]{3,0,2,1:T(8,128)(2,1)S(1)}, u32[]{:S(2)}, u32[]{:S(2)}) async-start(bf16[8,128,2,128]{3,0,2,1:T(8,128)(2,1)} %bitcast.21), calls=%async_computation.5 | async-start | bytes 1048576 | tf_op jit(solution)/shard_map/all_to_all | solution.py:129
  223.1 19.7 %reduce-scatter.3.cloned.1.call-done = bf16[8,256,128]{2,1,0:T(8,128)(2,1)} async-done(((bf16[8,1024,128]{2,1,0:T(8,128)(2,1)}), bf16[8,256,128]{2,1,0:T(8,128)(2,1)}) %reduce-scatter.3.cloned.1.call-update) | async-done | bytes 524304 | tf_op jit(solution)/shard_map/reduce_scatter | solution.py:118
  242.8 2.2 copy.131
  245.0 14.2 %all-to-all-start.6 = ((bf16[8,128,2,128]{3,0,2,1:T(8,128)(2,1)}), bf16[8,128,2,128]{3,0,2,1:T(8,128)(2,1)S(1)}, u32[]{:S(2)}, u32[]{:S(2)}) async-start(bf16[8,128,2,128]{3,0,2,1:T(8,128)(2,1)} %bitcast.25), calls=%async_computation.7 | async-start | bytes 1048576 | tf_op jit(solution)/shard_map/all_to_all | solution.py:130
  259.3 21.3 %reduce-scatter.5.cloned.1.call-done = bf16[8,256,128]{2,1,0:T(8,128)(2,1)} async-done(((bf16[8,1024,128]{2,1,0:T(8,128)(2,1)}), bf16[8,256,128]{2,1,0:T(8,128)(2,1)}) %reduce-scatter.5.cloned.1.call-update) | async-done | bytes 524304 | tf_op jit(solution)/shard_map/reduce_scatter | solution.py:121
  280.6 2.2 copy.133
  282.7 14.2 %all-to-all-start.7 = ((bf16[8,128,2,128]{3,0,2,1:T(8,128)(2,1)}), bf16[8,128,2,128]{3,0,2,1:T(8,128)(2,1)S(1)}, u32[]{:S(2)}, u32[]{:S(2)}) async-start(bf16[8,128,2,128]{3,0,2,1:T(8,128)(2,1)} %bitcast.29), calls=%async_computation.9 | async-start | bytes 1048576 | tf_op jit(solution)/shard_map/all_to_all | solution.py:131
  299.5 18.0 %all-to-all-done.7 = bf16[8,128,2,128]{3,0,2,1:T(8,128)(2,1)S(1)} async-done(((bf16[8,128,2,128]{3,0,2,1:T(8,128)(2,1)}), bf16[8,128,2,128]{3,0,2,1:T(8,128)(2,1)S(1)}, u32[]{:S(2)}, u32[]{:S(2)}) %all-to-all-start.7) | async-done | bytes 524320 | tf_op jit(solution)/shard_map/all_to_all | solution.py:131
  (147 shorter events, 35.3 us)
Async XLA Ops:
  7.2 1.9 copy-start
  7.2 141.6 %all-gather.5.cloned.1.call-start = ((), (), s32[]{:S(2)}) async-start(), calls=%async_computation.11 | async-start | bytes 2621440 | tf_op jit(solution)/shard_map/all_gather | solution.py:98
  9.0 40.4 %copy-start.2 = (bf16[128,1024]{1,0:T(8,128)(2,1)S(1)}, bf16[128,1024]{1,0:T(8,128)(2,1)}, u32[]{:S(2)}) copy-start(bf16[128,1024]{1,0:T(8,128)(2,1)} %param.8) | copy-start | bytes 786436
  49.4 101.2 %all-gather.3.cloned.1.call-start = ((), (), s32[]{:S(2)}) async-start(), calls=%async_computation.10 | async-start | bytes 2621440 | tf_op jit(solution)/shard_map/all_gather | solution.py:97
  49.8 33.8 %copy-start.3 = (bf16[128,1024]{1,0:T(8,128)(2,1)S(1)}, bf16[128,1024]{1,0:T(8,128)(2,1)}, u32[]{:S(2)}) copy-start(bf16[128,1024]{1,0:T(8,128)(2,1)} %param.10) | copy-start | bytes 786436
  76.9 25.0 %copy-start.4 = (bf16[128,1024]{1,0:T(8,128)(2,1)S(1)}, bf16[128,1024]{1,0:T(8,128)(2,1)}, u32[]{:S(2)}) copy-start(bf16[128,1024]{1,0:T(8,128)(2,1)} %param.7) | copy-start | bytes 786436
  78.2 18.1 %all-to-all-start = ((s32[8,128,2]{0,2,1:T(2,128)}), s32[8,128,2]{0,2,1:T(2,128)S(1)}, u32[]{:S(2)}, u32[]{:S(2)}) async-start(s32[8,128,2]{0,2,1:T(2,128)} %bitcast.11), calls=%async_computation | async-start | bytes 262144 | tf_op jit(solution)/shard_map/all_to_all | solution.py:83
  96.3 26.3 %all-to-all-start.3 = ((bf16[8,128,2,128]{3,0,2,1:T(8,128)(2,1)}), bf16[8,128,2,128]{3,0,2,1:T(8,128)(2,1)S(1)}, u32[]{:S(2)}, u32[]{:S(2)}) async-start(bf16[8,128,2,128]{3,0,2,1:T(8,128)(2,1)} %copy.119), calls=%async_computation.3 | async-start | bytes 1048576 | tf_op jit(solution)/shard_map/all_to_all | solution.py:82
  122.6 26.0 %all-to-all-start.1 = ((bf16[8,128,2,128]{3,2,0,1:T(2,128)(2,1)}), bf16[8,128,2,128]{3,2,0,1:T(2,128)(2,1)S(1)}, u32[]{:S(2)}, u32[]{:S(2)}) async-start(bf16[8,128,2,128]{3,2,0,1:T(2,128)(2,1)} %copy.113), calls=%async_computation.1 | async-start | bytes 1048576 | tf_op jit(solution)/shard_map/all_to_all | solution.py:79
  128.0 114.8 %reduce-scatter.3.cloned.1.call-start = ((), (), s32[]{:S(2)}) async-start(), calls=%async_computation.12 | async-start | bytes 2621440 | tf_op jit(solution)/shard_map/reduce_scatter | solution.py:118
  213.9 1.0 copy-start.1
  214.0 66.6 %reduce-scatter.5.cloned.1.call-start = ((), (), s32[]{:S(2)}) async-start(), calls=%async_computation.13 | async-start | bytes 2621440 | tf_op jit(solution)/shard_map/reduce_scatter | solution.py:121
  216.1 28.9 %all-to-all-start.5 = ((bf16[8,128,2,128]{3,0,2,1:T(8,128)(2,1)}), bf16[8,128,2,128]{3,0,2,1:T(8,128)(2,1)S(1)}, u32[]{:S(2)}, u32[]{:S(2)}) async-start(bf16[8,128,2,128]{3,0,2,1:T(8,128)(2,1)} %bitcast.21), calls=%async_computation.5 | async-start | bytes 1048576 | tf_op jit(solution)/shard_map/all_to_all | solution.py:129
  245.0 37.7 %all-to-all-start.6 = ((bf16[8,128,2,128]{3,0,2,1:T(8,128)(2,1)}), bf16[8,128,2,128]{3,0,2,1:T(8,128)(2,1)S(1)}, u32[]{:S(2)}, u32[]{:S(2)}) async-start(bf16[8,128,2,128]{3,0,2,1:T(8,128)(2,1)} %bitcast.25), calls=%async_computation.7 | async-start | bytes 1048576 | tf_op jit(solution)/shard_map/all_to_all | solution.py:130
  282.7 34.8 %all-to-all-start.7 = ((bf16[8,128,2,128]{3,0,2,1:T(8,128)(2,1)}), bf16[8,128,2,128]{3,0,2,1:T(8,128)(2,1)S(1)}, u32[]{:S(2)}, u32[]{:S(2)}) async-start(bf16[8,128,2,128]{3,0,2,1:T(8,128)(2,1)} %bitcast.29), calls=%async_computation.9 | async-start | bytes 1048576 | tf_op jit(solution)/shard_map/all_to_all | solution.py:131
Sparse Core Ops, SparseCore 0:
  49.6 28.6 all-gather.4
  80.3 36.2 all-gather.2
  214.1 28.6 reduce-scatter.2
  245.7 34.7 reduce-scatter.4
where the time goes:
time: 327 us; the launch traced here: 325 us
  waiting for transfers between devices  98 us (30%)
  blocking collectives  76.4 us (23%)
  starting transfers between devices  51.9 us (16%)
  matrix products  51.9 us (16%)
  local copies, waits for them, and re-layouts  20.3 us (6%)
  between operations  14 us (4%)
  other arithmetic  12.2 us (4%)
    all_to_all x1, blocking collectives, local(): lax.all_to_all(place(values), 'seq', split_axis=1, concat_axis=1, tiled=T...  38.8 us
    all_to_all x1, blocking collectives, local(): lax.all_to_all(place(keys), 'seq', split_axis=1, concat_axis=1, tiled=True)  25.8 us
    reduce_scatter x1, waiting for transfers between devices, local(): lax.psum_scatter(value_terms.astype(jnp.bfloat16), 'spill', scatter_dimen...  21.3 us
    reduce_scatter x1, waiting for transfers between devices, local(): lax.psum_scatter(key_terms.astype(jnp.bfloat16), 'spill', scatter_dimensi...  19.7 us
    all_to_all x1, waiting for transfers between devices, local(): lax.all_to_all(place(out_grad), 'seq', split_axis=1, concat_axis=1, tiled...  19.2 us
    all_to_all x1, waiting for transfers between devices, local(): lax.all_to_all(value_slots.reshape(shaped), 'seq', split_axis=1, concat_a...  18 us
    dot_general x16, matrix products, contract_first(): lax.dot_general(left, right, (((0,), (0,)), ((), ())), preferred_element_...  16.9 us
    dot_general x16, matrix products, contract_last(): lax.dot_general(left, right, (((1,), (1,)), ((), ())), preferred_element_...  15 us
  transfers between devices with their start and end apart: 10, of which 6 were waited for; matrix products, arithmetic and copies ran while one was open for 5% of the time, Pallas kernels for 0%

commit v1 on v0

v1 whole, which is shorter than its diff:
```python
import functools

import jax
import jax.numpy as jnp
from jax import lax
from jax.experimental import pallas as pl
from jax.experimental.pallas import tpu as pltpu
from jax.sharding import PartitionSpec as P

AXES = ("seq", "spill")
LANES = 128
SLOTS = 2
MASKED_SCORE = -1e30
LOWEST_MAX = -5e29


def dot(left, right):
    return jnp.dot(left, right, preferred_element_type=jnp.float32)


def dot_last(left, right):
    return lax.dot_general(
        left, right, (((1,), (1,)), ((), ())), preferred_element_type=jnp.float32
    )


def iota(rows, columns, axis):
    return lax.broadcasted_iota(jnp.int32, (rows, columns), axis)


def place_kernel(owners, spills, q_ref, k_ref, v_ref, g_ref, ids_ref, out_ref, rows_ref):
    tokens, heads = ids_ref.shape
    per_dest = heads // spills
    arrays = (q_ref, k_ref, v_ref, g_ref)
    data_rows = per_dest * len(arrays) * SLOTS
    message = data_rows + per_dest
    owner_iota = iota(owners, tokens, 0)
    earlier = (iota(tokens, tokens, 0) < iota(tokens, tokens, 1)).astype(jnp.bfloat16)
    first_lanes = iota(owners, LANES, 1) < LANES // 2
    for head in range(heads):
        dest, within = divmod(head, per_dest)
        id_column = ids_ref[:, head : head + 1].astype(jnp.float32)
        ids = jnp.transpose(jnp.broadcast_to(id_column, (tokens, owners))).astype(jnp.int32)
        hot = ids % owners == owner_iota
        count = dot(hot.astype(jnp.bfloat16), earlier)
        first = hot & (count < 0.5)
        second = hot & (count > 0.5)
        select = jnp.concatenate([first.astype(jnp.bfloat16), second.astype(jnp.bfloat16)], axis=0)
        columns = slice(head * LANES, (head + 1) * LANES)
        placed = dot(select, jnp.concatenate([ref[:, columns] for ref in arrays], axis=1))
        base = dest * message
        for array in range(len(arrays)):
            for slot in range(SLOTS):
                row = base + (within * len(arrays) + array) * SLOTS + slot
                rows_ref[pl.ds(row, owners, stride=spills * message), :] = placed[
                    slot * owners : (slot + 1) * owners, array * LANES : (array + 1) * LANES
                ]
        label = (ids // owners + 1).astype(jnp.float32)
        first_label = jnp.sum(jnp.where(first, label, 0.0), axis=1, keepdims=True)
        second_label = jnp.sum(jnp.where(second, label, 0.0), axis=1, keepdims=True)
        rows_ref[pl.ds(base + data_rows + within, owners, stride=spills * message), :] = jnp.where(
            first_lanes, first_label, second_label
        )
    out_ref[...] = rows_ref[...].astype(jnp.bfloat16)


def attend_kernel(per_dest, message, x_ref, out_ref, rows_ref, back_ref, q_s, k_s, v_s, g_s, dk_s, dv_s):
    blocks = x_ref.shape[0] // message
    back = back_ref.shape[0] // blocks
    groups = blocks // LANES
    tile = SLOTS * LANES
    scale = LANES ** (-0.5)
    arrays = (q_s, k_s, v_s, g_s)
    rows_ref[...] = x_ref[...].astype(jnp.float32)
    key_at = SLOTS * (iota(tile, tile, 0) % LANES) + iota(tile, tile, 0) // LANES
    query_at = SLOTS * (iota(tile, tile, 1) % LANES) + iota(tile, tile, 1) // LANES
    causal = key_at <= query_at
    for head in range(per_dest):
        key_labels, query_labels = [], []
        for group in range(groups):
            first_row = group * LANES * message
            for array, scratch in enumerate(arrays):
                for slot in range(SLOTS):
                    row = first_row + (head * len(arrays) + array) * SLOTS + slot
                    at = (group * SLOTS + slot) * LANES
                    scratch[at : at + LANES, :] = rows_ref[
                        pl.ds(row, LANES, stride=message), :
                    ].astype(jnp.bfloat16)
            row = first_row + per_dest * len(arrays) * SLOTS + head
            label = rows_ref[pl.ds(row, LANES, stride=message), :]
            turned = jnp.transpose(label)
            half = LANES // 2
            key_labels.append(jnp.concatenate([label[:, :1], label[:, half : half + 1]], axis=0))
            row_label = jnp.concatenate([turned[:1, :], turned[half : half + 1, :]], axis=1)
            query_labels.append(jnp.where(row_label > 0.5, row_label, -1.0))
        dk_s[...] = jnp.zeros_like(dk_s)
        dv_s[...] = jnp.zeros_like(dv_s)
        for query_group in range(groups):
            own = slice(query_group * tile, (query_group + 1) * tile)
            q_rows, g_rows = q_s[own, :], g_s[own, :]
            scores = []
            row_max = jnp.full((1, tile), LOWEST_MAX, jnp.float32)
            for key_group in range(query_group + 1):
                keys = slice(key_group * tile, (key_group + 1) * tile)
                allowed = key_labels[key_group] == query_labels[query_group]
                if key_group == query_group:
                    allowed = allowed & causal
                score = jnp.where(allowed, dot_last(k_s[keys, :], q_rows) * scale, MASKED_SCORE)
                row_max = jnp.maximum(row_max, jnp.max(score, axis=0, keepdims=True))
                scores.append(score)
            total = jnp.zeros((1, tile), jnp.float32)
            weighted = jnp.zeros((1, tile), jnp.float32)
            raw, grads = [], []
            for key_group in range(query_group + 1):
                keys = slice(key_group * tile, (key_group + 1) * tile)
                weight = jnp.exp(scores[key_group] - row_max)
                prob_grad = dot_last(v_s[keys, :], g_rows)
                total = total + jnp.sum(weight, axis=0, keepdims=True)
                weighted = weighted + jnp.sum(weight * prob_grad, axis=0, keepdims=True)
                raw.append(weight)
                grads.append(prob_grad)
            inverse = 1.0 / jnp.maximum(total, 1.0)
            delta = weighted * inverse
            query_grad = jnp.zeros((LANES, tile), jnp.float32)
            for key_group in range(query_group + 1):
                keys = slice(key_group * tile, (key_group + 1) * tile)
                prob = raw[key_group] * inverse
                score_grad = (prob * (grads[key_group] - delta) * scale).astype(jnp.bfloat16)
                dv_s[keys, :] += dot(prob.astype(jnp.bfloat16), g_rows)
                dk_s[keys, :] += dot(score_grad, q_rows)
                query_grad = query_grad + lax.dot_general(
                    k_s[keys, :],
                    score_grad,
                    (((0,), (0,)), ((), ())),
                    preferred_element_type=jnp.float32,
                )
            query_rows = jnp.transpose(query_grad)
            for slot in range(SLOTS):
                row = query_group * LANES * back + head * 3 * SLOTS + slot
                back_ref[pl.ds(row, LANES, stride=back), :] = query_rows[
                    slot * LANES : (slot + 1) * LANES, :
                ]
        for array, grad in ((1, dk_s), (2, dv_s)):
            for group in range(groups):
                for slot in range(SLOTS):
                    row = group * LANES * back + (head * 3 + array) * SLOTS + slot
                    at = (group * SLOTS + slot) * LANES
                    back_ref[pl.ds(row, LANES, stride=back), :] = grad[at : at + LANES, :]
    out_ref[...] = back_ref[...].astype(jnp.bfloat16)


def unplace_kernel(owners, spills, y_ref, ids_ref, dq_ref, dk_ref, dv_ref, rows_ref):
    tokens, heads = ids_ref.shape
    per_dest = heads // spills
    outs = (dq_ref, dk_ref, dv_ref)
    back = per_dest * len(outs) * SLOTS
    owner_iota = iota(tokens, owners, 1)
    earlier = (iota(tokens, tokens, 1) < iota(tokens, tokens, 0)).astype(jnp.bfloat16)
    rows_ref[...] = y_ref[...].astype(jnp.float32)
    for head in range(heads):
        dest, within = divmod(head, per_dest)
        hot = ids_ref[:, head : head + 1] % owners == owner_iota
        count = dot(earlier, hot.astype(jnp.bfloat16))
        first = hot & (count < 0.5)
        second = hot & (count > 0.5)
        select = jnp.concatenate([first.astype(jnp.bfloat16), second.astype(jnp.bfloat16)], axis=1)
        stacked = []
        for array in range(len(outs)):
            slots = []
            for slot in range(SLOTS):
                row = dest * back + (within * len(outs) + array) * SLOTS + slot
                slots.append(rows_ref[pl.ds(row, owners, stride=spills * back), :])
            stacked.append(jnp.concatenate(slots, axis=0).astype(jnp.bfloat16))
        result = dot(select, jnp.concatenate(stacked, axis=1)).astype(jnp.bfloat16)
        for array, ref in enumerate(outs):
            ref[:, head * LANES : (head + 1) * LANES] = result[:, array * LANES : (array + 1) * LANES]


def local(queries, keys, values, out_grad, cluster_ids):
    tokens, width = queries.shape
    heads = cluster_ids.shape[1]
    owners = lax.axis_size("seq")
    spills = lax.axis_size("spill")
    devices = owners * spills
    per_dest = heads // spills
    message = per_dest * (4 * SLOTS + 1)
    back = per_dest * 3 * SLOTS
    whole = pl.BlockSpec(memory_space=pltpu.VMEM)
    params = pltpu.CompilerParams(vmem_limit_bytes=48 * 1024 * 1024)

    def exchange(rows, count):
        cut = rows.reshape(devices, count // SLOTS, SLOTS, LANES)
        moved = lax.all_to_all(cut, AXES, split_axis=0, concat_axis=0, tiled=True)
        return moved.reshape(devices * count, LANES)

    placed = pl.pallas_call(
        functools.partial(place_kernel, owners, spills),
        out_shape=jax.ShapeDtypeStruct((devices * message, LANES), jnp.bfloat16),
        in_specs=[whole] * 5,
        out_specs=whole,
        scratch_shapes=[pltpu.VMEM((devices * message, LANES), jnp.float32)],
        compiler_params=params,
        name="place",
    )(queries, keys, values, out_grad, cluster_ids)
    routed = exchange(placed, message)
    slots = devices * SLOTS
    returned = pl.pallas_call(
        functools.partial(attend_kernel, per_dest, message),
        out_shape=jax.ShapeDtypeStruct((devices * back, LANES), jnp.bfloat16),
        in_specs=[whole],
        out_specs=whole,
        scratch_shapes=[
            pltpu.VMEM((devices * message, LANES), jnp.float32),
            pltpu.VMEM((devices * back, LANES), jnp.float32),
        ]
        + [pltpu.VMEM((slots, LANES), jnp.bfloat16)] * 4
        + [pltpu.VMEM((slots, LANES), jnp.float32)] * 2,
        compiler_params=params,
        name="attend",
    )(routed)
    gradients = exchange(returned, back)
    grad_shape = jax.ShapeDtypeStruct((tokens, width), jnp.bfloat16)
    return pl.pallas_call(
        functools.partial(unplace_kernel, owners, spills),
        out_shape=(grad_shape, grad_shape, grad_shape),
        in_specs=[whole] * 2,
        out_specs=(whole, whole, whole),
        scratch_shapes=[pltpu.VMEM((devices * back, LANES), jnp.float32)],
        compiler_params=params,
        name="unplace",
    )(gradients, cluster_ids)


def solution(mesh):
    rows = P(AXES, None)
    return jax.shard_map(
        local,
        mesh=mesh,
        in_specs=(rows, rows, rows, rows, rows),
        out_specs=(rows, rows, rows),
        check_vma=False,
    )
```

time: 327 us -> 152 us (0.46)
  waiting for transfers between devices: 98 us -> 0 us
  blocking collectives: 76.4 us -> 134 us
  matrix products: 51.9 us -> 0 us
  starting transfers between devices: 51.9 us -> 0 us
  local copies, waits for them, and re-layouts: 20.3 us -> 4.58 us
  between operations: 14 us -> 0.66 us
  other arithmetic: 12.2 us -> 0 us
  Pallas kernels: 0 us -> 11.5 us
    all_to_all x2, blocking collectives: 64.6 us -> 134 us  [exchange(): moved = lax.all_to_all(cut, AXES, split_axis=0, concat_axis=0, tiled=True)]
    all_to_all x6 -> x0, waiting for transfers between devices: 56.4 us -> none  [the longest x1 19.2 us: local(): lax.all_to_all(place(out_grad), 'seq', split_axis=1, concat_axis=1, tiled...]
    dot_general x55 -> x0, matrix products: 51.9 us -> none  [the longest x16 16.9 us: contract_first(): lax.dot_general(left, right, (((0,), (0,)), ((), ())), preferred_element_...]
    all_to_all x6 -> x0, starting transfers between devices: 51.8 us -> none  [the longest x1 14.2 us: local(): lax.all_to_all(key_slots.reshape(shaped), 'seq', split_axis=1, concat_axi...]
    reduce_scatter x2 -> x0, waiting for transfers between devices: 41 us -> none  [the longest x1 21.3 us: local(): lax.psum_scatter(value_terms.astype(jnp.bfloat16), 'spill', scatter_dimen...]
    all_gather x1 -> x0, blocking collectives: 11.8 us -> none  [local(): lax.all_gather(for_sending(label_slots), 'spill', axis=1, tiled=True)]
    pallas_call x0 -> x3, Pallas kernels: none -> 11.5 us  [the longest x1 6.46 us: local(): pl.pallas_call(functools.partial(attend_kernel, per_dest, message), out_s...]
    while x7 -> x0, local copies, waits for them, and re-layouts: 6.83 us -> none  [local(): lax.map(per_head_keys, (q_slots, g_slots, label_slots, k_group, v_group,...]
  transfers between devices with their start and end apart: 10 -> 0, of which waited for: 6 -> 0; matrix products, arithmetic and copies ran while one was open for 5% -> 0% of each run, Pallas kernels for 0% -> 0%
where the time goes in v1:
time: 152 us; the launch traced here: 151 us
  blocking collectives  134 us (88%)
  Pallas kernels  11.5 us (8%)
  local copies, waits for them, and re-layouts  4.58 us (3%)
    all_to_all x2, blocking collectives, exchange(): moved = lax.all_to_all(cut, AXES, split_axis=0, concat_axis=0, tiled=True)  134 us
    pallas_call x1, Pallas kernels, local(): pl.pallas_call(functools.partial(attend_kernel, per_dest, message), out_s...  6.46 us
    unnamed x9, local copies, waits for them, and re-layouts  4.58 us

profile of v1, /device:TPU:1, one launch (start us, length us, event | category | flops | bytes accessed | tf_op | source)
XLA Modules:
  0.0 151.2 jit_solution(10881582665587212087)
XLA Ops:
  0.6 0.8 copy.8.ids_ref
  1.4 0.0 copy-start
  1.4 0.9 copy-done
  2.4 0.0 copy-start.1
  2.4 0.9 copy-done.1
  3.3 0.0 copy-start.2
  3.3 0.9 copy-done.2
  4.3 0.0 copy-start.3
  4.3 0.9 copy-done.3
  5.2 2.4 %place.1 = bf16[9216,128]{1,0:T(8,128)(2,1)S(1)} custom-call(bf16[128,1024]{1,0:T(8,128)(2,1)S(1)} %copy-done, bf16[128,1024]{1,0:T(8,128)(2,1)S(1)} %copy-done.1, bf16[128,1024]{1,0:T(8,128)(2,1)S(1)} %copy-done.2, bf16[128,1024]{1,0:T(8,128)(2,1)S(1)} %copy-done.3, s32[128,8]{1,0:T(8,128)S(1)} %copy.8.ids_ref), custom_call_target="tpu_custom_call" | custom-call | tf_op jit(solution)/shard_map/place/pallas_call | solution.py:196
  7.6 81.7 %all_to_all.10 = bf16[512,9,2,128]{3,2,1,0:T(2,128)(2,1)S(1)} all-to-all(bf16[512,9,2,128]{3,2,1,0:T(2,128)(2,1)S(1)} %bitcast.5), channel_id=1, replica_groups=mesh['seq'=128,'spill'=4] {'seq','spill'}, dimensions={0} | all-to-all | bytes 4718592 | tf_op jit(solution)/shard_map/all_to_all | solution.py:193
  89.3 6.5 %attend.1 = bf16[6144,128]{1,0:T(8,128)(2,1)S(1)} custom-call(bf16[9216,128]{1,0:T(8,128)(2,1)S(1)} %bitcast.4), custom_call_target="tpu_custom_call" | custom-call | tf_op jit(solution)/shard_map/attend/pallas_call | solution.py:207
  95.8 52.7 %all_to_all.11 = bf16[512,6,2,128]{3,2,1,0:T(2,128)(2,1)S(1)} all-to-all(bf16[512,6,2,128]{3,2,1,0:T(2,128)(2,1)S(1)} %bitcast.7), channel_id=1, replica_groups=mesh['seq'=128,'spill'=4] {'seq','spill'}, dimensions={0} | all-to-all | bytes 3145728 | tf_op jit(solution)/shard_map/all_to_all | solution.py:193
  148.5 2.6 %unplace.1 = (bf16[128,1024]{1,0:T(8,128)(2,1)}, bf16[128,1024]{1,0:T(8,128)(2,1)}, bf16[128,1024]{1,0:T(8,128)(2,1)}) custom-call(bf16[6144,128]{1,0:T(8,128)(2,1)S(1)} %bitcast.6, s32[128,8]{1,0:T(8,128)S(1)} %copy.8.ids_ref), custom_call_target="tpu_custom_call" | custom-call | tf_op jit(solution)/shard_map/unplace/pallas_call | solution.py:223
Async XLA Ops:
  1.4 0.9 copy-start
  2.4 0.9 copy-start.1
  3.3 0.9 copy-start.2
  4.3 0.9 copy-start.3

commit v2 on v1

--- a/solution.py
+++ b/solution.py
@@ -1,4 +1,5 @@
 import functools
+import math
 
 import jax
 import jax.numpy as jnp
@@ -12,6 +13,7 @@
 SLOTS = 2
 MASKED_SCORE = -1e30
 LOWEST_MAX = -5e29
+LOG2_E = math.log2(math.e)
 
 
 def dot(left, right):
@@ -28,39 +30,58 @@
     return lax.broadcasted_iota(jnp.int32, (rows, columns), axis)
 
 
-def place_kernel(owners, spills, q_ref, k_ref, v_ref, g_ref, ids_ref, out_ref, rows_ref):
-    tokens, heads = ids_ref.shape
+def choose(ids, owners, earlier):
+    ids = jnp.broadcast_to(ids, (owners, ids.shape[1]))
+    hot = ids % owners == iota(owners, ids.shape[1], 0)
+    count = dot(hot.astype(jnp.bfloat16), earlier)
+    return hot & (count < 0.5), hot & (count > 0.5), (ids // owners + 1).astype(jnp.float32)
+
+
+def place_kernel(
+    owners, spills, q_hbm, k_hbm, v_hbm, g_hbm, ids_hbm, out_ref, q_ref, k_ref, v_ref, g_ref, ids_ref, rows_ref, sems
+):
+    heads, tokens = ids_ref.shape
+    ids_copy = pltpu.make_async_copy(ids_hbm, ids_ref, sems.at[4 * spills])
+    ids_copy.start()
     per_dest = heads // spills
+    width = per_dest * LANES
     arrays = (q_ref, k_ref, v_ref, g_ref)
+    copies = []
+    for dest in range(spills):
+        columns = slice(dest * width, (dest + 1) * width)
+        for array, (source, target) in enumerate(zip((q_hbm, k_hbm, v_hbm, g_hbm), arrays)):
+            copies.append(
+                pltpu.make_async_copy(
+                    source.at[:, columns], target.at[:, columns], sems.at[dest * len(arrays) + array]
+                )
+            )
+            copies[-1].start()
     data_rows = per_dest * len(arrays) * SLOTS
     message = data_rows + per_dest
-    owner_iota = iota(owners, tokens, 0)
     earlier = (iota(tokens, tokens, 0) < iota(tokens, tokens, 1)).astype(jnp.bfloat16)
     first_lanes = iota(owners, LANES, 1) < LANES // 2
+    ids_copy.wait()
     for head in range(heads):
         dest, within = divmod(head, per_dest)
-        id_column = ids_ref[:, head : head + 1].astype(jnp.float32)
-        ids = jnp.transpose(jnp.broadcast_to(id_column, (tokens, owners))).astype(jnp.int32)
-        hot = ids % owners == owner_iota
-        count = dot(hot.astype(jnp.bfloat16), earlier)
-        first = hot & (count < 0.5)
-        second = hot & (count > 0.5)
+        first, second, label = choose(ids_ref[head : head + 1, :], owners, earlier)
         select = jnp.concatenate([first.astype(jnp.bfloat16), second.astype(jnp.bfloat16)], axis=0)
+        base = dest * message
+        first_label = jnp.sum(jnp.where(first, label, 0.0), axis=1, keepdims=True)
+        second_label = jnp.sum(jnp.where(second, label, 0.0), axis=1, keepdims=True)
+        rows_ref[pl.ds(base + data_rows + within, owners, stride=spills * message), :] = jnp.where(
+            first_lanes, first_label, second_label
+        )
+        if within == 0:
+            for copy in copies[dest * len(arrays) : (dest + 1) * len(arrays)]:
+                copy.wait()
         columns = slice(head * LANES, (head + 1) * LANES)
         placed = dot(select, jnp.concatenate([ref[:, columns] for ref in arrays], axis=1))
-        base = dest * message
         for array in range(len(arrays)):
             for slot in range(SLOTS):
                 row = base + (within * len(arrays) + array) * SLOTS + slot
                 rows_ref[pl.ds(row, owners, stride=spills * message), :] = placed[
                     slot * owners : (slot + 1) * owners, array * LANES : (array + 1) * LANES
                 ]
-        label = (ids // owners + 1).astype(jnp.float32)
-        first_label = jnp.sum(jnp.where(first, label, 0.0), axis=1, keepdims=True)
-        second_label = jnp.sum(jnp.where(second, label, 0.0), axis=1, keepdims=True)
-        rows_ref[pl.ds(base + data_rows + within, owners, stride=spills * message), :] = jnp.where(
-            first_lanes, first_label, second_label
-        )
     out_ref[...] = rows_ref[...].astype(jnp.bfloat16)
 
 
@@ -105,7 +126,7 @@
                 allowed = key_labels[key_group] == query_labels[query_group]
                 if key_group == query_group:
                     allowed = allowed & causal
-                score = jnp.where(allowed, dot_last(k_s[keys, :], q_rows) * scale, MASKED_SCORE)
+                score = jnp.where(allowed, dot_last(k_s[keys, :], q_rows), MASKED_SCORE)
                 row_max = jnp.maximum(row_max, jnp.max(score, axis=0, keepdims=True))
                 scores.append(score)
             total = jnp.zeros((1, tile), jnp.float32)
@@ -113,7 +134,7 @@
             raw, grads = [], []
             for key_group in range(query_group + 1):
                 keys = slice(key_group * tile, (key_group + 1) * tile)
-                weight = jnp.exp(scores[key_group] - row_max)
+                weight = jnp.exp2((scores[key_group] - row_max) * (scale * LOG2_E))
                 prob_grad = dot_last(v_s[keys, :], g_rows)
                 total = total + jnp.sum(weight, axis=0, keepdims=True)
                 weighted = weighted + jnp.sum(weight * prob_grad, axis=0, keepdims=True)
@@ -125,7 +146,7 @@
             for key_group in range(query_group + 1):
                 keys = slice(key_group * tile, (key_group + 1) * tile)
                 prob = raw[key_group] * inverse
-                score_grad = (prob * (grads[key_group] - delta) * scale).astype(jnp.bfloat16)
+                score_grad = (prob * (grads[key_group] - delta)).astype(jnp.bfloat16)
                 dv_s[keys, :] += dot(prob.astype(jnp.bfloat16), g_rows)
                 dk_s[keys, :] += dot(score_grad, q_rows)
                 query_grad = query_grad + lax.dot_general(
@@ -134,32 +155,35 @@
                     (((0,), (0,)), ((), ())),
                     preferred_element_type=jnp.float32,
                 )
-            query_rows = jnp.transpose(query_grad)
+            query_rows = jnp.transpose(query_grad) * scale
             for slot in range(SLOTS):
                 row = query_group * LANES * back + head * 3 * SLOTS + slot
                 back_ref[pl.ds(row, LANES, stride=back), :] = query_rows[
                     slot * LANES : (slot + 1) * LANES, :
                 ]
-        for array, grad in ((1, dk_s), (2, dv_s)):
+        for array, grad, factor in ((1, dk_s, scale), (2, dv_s, 1.0)):
             for group in range(groups):
                 for slot in range(SLOTS):
                     row = group * LANES * back + (head * 3 + array) * SLOTS + slot
                     at = (group * SLOTS + slot) * LANES
-                    back_ref[pl.ds(row, LANES, stride=back), :] = grad[at : at + LANES, :]
+                    back_ref[pl.ds(row, LANES, stride=back), :] = grad[at : at + LANES, :] * factor
     out_ref[...] = back_ref[...].astype(jnp.bfloat16)
 
 
-def unplace_kernel(owners, spills, y_ref, ids_ref, dq_ref, dk_ref, dv_ref, rows_ref):
-    tokens, heads = ids_ref.shape
+def unplace_kernel(owners, spills, y_ref, ids_ref, dq_hbm, dk_hbm, dv_hbm, rows_ref, dq_ref, dk_ref, dv_ref, sems):
+    heads, tokens = ids_ref.shape
     per_dest = heads // spills
+    width = per_dest * LANES
     outs = (dq_ref, dk_ref, dv_ref)
     back = per_dest * len(outs) * SLOTS
     owner_iota = iota(tokens, owners, 1)
     earlier = (iota(tokens, tokens, 1) < iota(tokens, tokens, 0)).astype(jnp.bfloat16)
+    ids = jnp.transpose(ids_ref[...].astype(jnp.float32)).astype(jnp.int32)
     rows_ref[...] = y_ref[...].astype(jnp.float32)
+    copies = []
     for head in range(heads):
         dest, within = divmod(head, per_dest)
-        hot = ids_ref[:, head : head + 1] % owners == owner_iota
+        hot = ids[:, head : head + 1] % owners == owner_iota
         count = dot(earlier, hot.astype(jnp.bfloat16))
         first = hot & (count < 0.5)
         second = hot & (count > 0.5)
@@ -174,37 +198,46 @@
         result = dot(select, jnp.concatenate(stacked, axis=1)).astype(jnp.bfloat16)
         for array, ref in enumerate(outs):
             ref[:, head * LANES : (head + 1) * LANES] = result[:, array * LANES : (array + 1) * LANES]
-
-
-def local(queries, keys, values, out_grad, cluster_ids):
-    tokens, width = queries.shape
-    heads = cluster_ids.shape[1]
-    owners = lax.axis_size("seq")
-    spills = lax.axis_size("spill")
+        if within == per_dest - 1:
+            columns = slice(dest * width, (dest + 1) * width)
+            for array, (source, target) in enumerate(zip(outs, (dq_hbm, dk_hbm, dv_hbm))):
+                copies.append(
+                    pltpu.make_async_copy(
+                        source.at[:, columns], target.at[:, columns], sems.at[dest * len(outs) + array]
+                    )
+                )
+                copies[-1].start()
+    for copy in copies:
+        copy.wait()
+
+
+def local_ops(owners, spills, tokens, heads):
     devices = owners * spills
     per_dest = heads // spills
     message = per_dest * (4 * SLOTS + 1)
     back = per_dest * 3 * SLOTS
+    slots = devices * SLOTS
+    width = heads * LANES
     whole = pl.BlockSpec(memory_space=pltpu.VMEM)
+    hbm = pl.BlockSpec(memory_space=pltpu.HBM)
     params = pltpu.CompilerParams(vmem_limit_bytes=48 * 1024 * 1024)
-
-    def exchange(rows, count):
-        cut = rows.reshape(devices, count // SLOTS, SLOTS, LANES)
-        moved = lax.all_to_all(cut, AXES, split_axis=0, concat_axis=0, tiled=True)
-        return moved.reshape(devices * count, LANES)
-
-    placed = pl.pallas_call(
+    token_rows = pltpu.VMEM((tokens, width), jnp.bfloat16)
+    grad_shape = jax.ShapeDtypeStruct((tokens, width), jnp.bfloat16)
+    place = pl.pallas_call(
         functools.partial(place_kernel, owners, spills),
         out_shape=jax.ShapeDtypeStruct((devices * message, LANES), jnp.bfloat16),
-        in_specs=[whole] * 5,
+        in_specs=[hbm] * 5,
         out_specs=whole,
-        scratch_shapes=[pltpu.VMEM((devices * message, LANES), jnp.float32)],
+        scratch_shapes=[token_rows] * 4
+        + [
+            pltpu.VMEM((heads, tokens), jnp.int32),
+            pltpu.VMEM((devices * message, LANES), jnp.float32),
+            pltpu.SemaphoreType.DMA((4 * spills + 1,)),
+        ],
         compiler_params=params,
         name="place",
-    )(queries, keys, values, out_grad, cluster_ids)
-    routed = exchange(placed, message)
-    slots = devices * SLOTS
-    returned = pl.pallas_call(
+    )
+    attend = pl.pallas_call(
         functools.partial(attend_kernel, per_dest, message),
         out_shape=jax.ShapeDtypeStruct((devices * back, LANES), jnp.bfloat16),
         in_specs=[whole],
@@ -217,18 +250,35 @@
         + [pltpu.VMEM((slots, LANES), jnp.float32)] * 2,
         compiler_params=params,
         name="attend",
-    )(routed)
-    gradients = exchange(returned, back)
-    grad_shape = jax.ShapeDtypeStruct((tokens, width), jnp.bfloat16)
-    return pl.pallas_call(
+    )
+    unplace = pl.pallas_call(
         functools.partial(unplace_kernel, owners, spills),
         out_shape=(grad_shape, grad_shape, grad_shape),
         in_specs=[whole] * 2,
-        out_specs=(whole, whole, whole),
-        scratch_shapes=[pltpu.VMEM((devices * back, LANES), jnp.float32)],
+        out_specs=(hbm, hbm, hbm),
+        scratch_shapes=[pltpu.VMEM((devices * back, LANES), jnp.float32)]
+        + [token_rows] * 3
+        + [pltpu.SemaphoreType.DMA((3 * spills,))],
         compiler_params=params,
         name="unplace",
-    )(gradients, cluster_ids)
+    )
+    return place, attend, unplace
+
+
+def local(queries, keys, values, out_grad, cluster_ids):
+    owners, spills = lax.axis_size("seq"), lax.axis_size("spill")
+    devices = owners * spills
+    place, attend, unplace = local_ops(owners, spills, *cluster_ids.shape)
+
+    def exchange(rows):
+        cut = rows.reshape(devices, -1, SLOTS, LANES)
+        moved = lax.all_to_all(cut, AXES, split_axis=0, concat_axis=0, tiled=True)
+        return moved.reshape(rows.shape)
+
+    ids = jnp.transpose(cluster_ids)
+    inputs = (queries, keys, values, out_grad, ids)
+    routed = exchange(place(*(pltpu.with_memory_space_constraint(x, pltpu.HBM) for x in inputs)))
+    return unplace(exchange(attend(routed)), ids)
 
 
 def solution(mesh):

time: 152 us -> 148 us (0.974)
  local copies, waits for them, and re-layouts: 4.58 us -> 0.01 us
    unnamed x9 -> x2, local copies, waits for them, and re-layouts: 4.58 us -> 0.01 us
where the time goes in v2:
time: 148 us
  blocking collectives  134 us (91%)
  Pallas kernels  12.3 us (8%)
    all_to_all x2, blocking collectives, exchange(): moved = lax.all_to_all(cut, AXES, split_axis=0, concat_axis=0, tiled=True)  134 us
    pallas_call x2, Pallas kernels, local(): return unplace(exchange(attend(routed)), ids)  8.88 us
    pallas_call x1, Pallas kernels, local(): place(*(pltpu.with_memory_space_constraint(x, pltpu.HBM) for x in inputs))  3.41 us

profile of v2, /device:TPU:1, one launch (start us, length us, event | category | flops | bytes accessed | tf_op | source)
XLA Modules:
  0.0 147.6 jit_solution(11958268216938535481)
XLA Ops:
  0.6 3.4 %place.1 = bf16[9216,128]{1,0:T(8,128)(2,1)S(1)} custom-call(bf16[128,1024]{1,0:T(8,128)(2,1)} %q_hbm.1, bf16[128,1024]{1,0:T(8,128)(2,1)} %k_hbm.1, bf16[128,1024]{1,0:T(8,128)(2,1)} %v_hbm.1, bf16[128,1024]{1,0:T(8,128)(2,1)} %g_hbm.1, s32[8,128]{1,0:T(8,128)} %bitcast.9), custom_call_target="tpu_custom_call" | custom-call | tf_op jit(solution)/shard_map/place/pallas_call | solution.py:280
  4.0 81.7 %all_to_all.10 = bf16[512,9,2,128]{3,2,1,0:T(2,128)(2,1)S(1)} all-to-all(bf16[512,9,2,128]{3,2,1,0:T(2,128)(2,1)S(1)} %bitcast.6), channel_id=1, replica_groups=mesh['seq'=128,'spill'=4] {'seq','spill'}, dimensions={0} | all-to-all | bytes 4718592 | tf_op jit(solution)/shard_map/all_to_all | solution.py:275
  85.8 6.3 %attend.1 = bf16[6144,128]{1,0:T(8,128)(2,1)S(1)} custom-call(bf16[9216,128]{1,0:T(8,128)(2,1)S(1)} %bitcast.5), custom_call_target="tpu_custom_call" | custom-call | tf_op jit(solution)/shard_map/attend/pallas_call | solution.py:281
  92.1 0.0 copy-start
  92.1 52.7 %all_to_all.11 = bf16[512,6,2,128]{3,2,1,0:T(2,128)(2,1)S(1)} all-to-all(bf16[512,6,2,128]{3,2,1,0:T(2,128)(2,1)S(1)} %bitcast.8), channel_id=1, replica_groups=mesh['seq'=128,'spill'=4] {'seq','spill'}, dimensions={0} | all-to-all | bytes 3145728 | tf_op jit(solution)/shard_map/all_to_all | solution.py:275
  144.8 0.0 copy-done
  144.8 2.6 %unplace.1 = (bf16[128,1024]{1,0:T(8,128)(2,1)}, bf16[128,1024]{1,0:T(8,128)(2,1)}, bf16[128,1024]{1,0:T(8,128)(2,1)}) custom-call(bf16[6144,128]{1,0:T(8,128)(2,1)S(1)} %bitcast.7, s32[8,128]{1,0:T(8,128)S(1)} %bitcast.10), custom_call_target="tpu_custom_call" | custom-call | tf_op jit(solution)/shard_map/unplace/pallas_call | solution.py:281
Async XLA Ops:
  92.1 52.8 %copy-start = (s32[128,8]{0,1:T(8,128)S(1)}, s32[128,8]{0,1:T(8,128)}, u32[]{:S(2)}) copy-start(s32[128,8]{0,1:T(8,128)} %param.9) | copy-start | bytes 12292

commit v3 on v2

v3 whole, which is shorter than its diff:
```python
import functools
import math

import jax
import jax.numpy as jnp
from jax import lax
from jax.experimental import pallas as pl
from jax.experimental.pallas import tpu as pltpu
from jax.sharding import PartitionSpec as P

AXES = ("seq", "spill")
LANES = 128
SLOTS = 2
FOLD = 8
MASKED_SCORE = -1e30
LOWEST_MAX = -5e29
LOG2_E = math.log2(math.e)


def dot(left, right):
    return jnp.dot(left, right, preferred_element_type=jnp.float32)


def dot_last(left, right):
    return lax.dot_general(
        left, right, (((1,), (1,)), ((), ())), preferred_element_type=jnp.float32
    )


def iota(rows, columns, axis):
    return lax.broadcasted_iota(jnp.int32, (rows, columns), axis)


def one_hot_pair(hot, count, axis):
    first = jnp.where(hot & (count < 0.5), 1.0, 0.0)
    second = jnp.where(hot & (count > 0.5), 1.0, 0.0)
    return first, second, jnp.concatenate([first, second], axis=axis).astype(jnp.bfloat16)


def place_kernel(
    owners,
    spills,
    q_hbm,
    k_hbm,
    v_hbm,
    g_hbm,
    ids_hbm,
    out_ref,
    return_ref,
    q_ref,
    k_ref,
    v_ref,
    g_ref,
    ids_ref,
    select_ref,
    rows_ref,
    sems,
):
    heads, tokens = ids_ref.shape
    per_dest = heads // spills
    width = per_dest * LANES
    arrays = (q_ref, k_ref, v_ref, g_ref)
    ids_copy = pltpu.make_async_copy(ids_hbm, ids_ref, sems.at[len(arrays) * spills])
    ids_copy.start()
    copies = []
    for dest in range(spills):
        columns = slice(dest * width, (dest + 1) * width)
        for array, (source, target) in enumerate(zip((q_hbm, k_hbm, v_hbm, g_hbm), arrays)):
            copies.append(
                pltpu.make_async_copy(
                    source.at[:, columns], target.at[:, columns], sems.at[dest * len(arrays) + array]
                )
            )
            copies[-1].start()
    data_rows = per_dest * len(arrays) * SLOTS
    message = data_rows + SLOTS
    token_before = iota(tokens, tokens, 0) < iota(tokens, tokens, 1)
    before = jnp.where(token_before, 1.0, 0.0).astype(jnp.bfloat16)
    after = jnp.where(iota(tokens, tokens, 1) < iota(tokens, tokens, 0), 1.0, 0.0).astype(jnp.bfloat16)
    half_lanes = iota(owners, LANES, 1) // (LANES // per_dest)
    ids_copy.wait()
    id_columns = jnp.transpose(ids_ref[...].astype(jnp.float32)).astype(jnp.int32)
    for dest in range(spills):
        slot_labels = [jnp.zeros((owners, LANES), jnp.float32)] * SLOTS
        for within in range(per_dest):
            head = dest * per_dest + within
            ids = jnp.broadcast_to(ids_ref[head : head + 1, :], (owners, tokens))
            hot = ids % owners == iota(owners, tokens, 0)
            count = dot(jnp.where(hot, 1.0, 0.0).astype(jnp.bfloat16), before)
            first, second, select = one_hot_pair(hot, count, 0)
            select_ref[head * SLOTS * owners : (head + 1) * SLOTS * owners, :] = select
            label = (ids // owners + 1).astype(jnp.float32)
            for slot, mask in enumerate((first, second)):
                slot_label = jnp.sum(mask * label, axis=1, keepdims=True)
                slot_labels[slot] = jnp.where(half_lanes == within, slot_label, slot_labels[slot])
            hot = id_columns[:, head : head + 1] % owners == iota(tokens, owners, 1)
            count = dot(after, jnp.where(hot, 1.0, 0.0).astype(jnp.bfloat16))
            return_ref[head * tokens : (head + 1) * tokens, :] = one_hot_pair(hot, count, 1)[2]
        for slot in range(SLOTS):
            row = dest * message + data_rows + slot
            rows_ref[pl.ds(row, owners, stride=spills * message), :] = slot_labels[slot]
    for head in range(heads):
        dest, within = divmod(head, per_dest)
        if within == 0:
            for copy in copies[dest * len(arrays) : (dest + 1) * len(arrays)]:
                copy.wait()
        columns = slice(head * LANES, (head + 1) * LANES)
        placed = dot(
            select_ref[head * SLOTS * owners : (head + 1) * SLOTS * owners, :],
            jnp.concatenate([ref[:, columns] for ref in arrays], axis=1),
        )
        for array in range(len(arrays)):
            for slot in range(SLOTS):
                row = dest * message + (within * len(arrays) + array) * SLOTS + slot
                rows_ref[pl.ds(row, owners, stride=spills * message), :] = placed[
                    slot * owners : (slot + 1) * owners, array * LANES : (array + 1) * LANES
                ]
    out_ref[...] = rows_ref[...].astype(jnp.bfloat16)


def attend_kernel(
    per_dest, message, x_ref, out_ref, rows_ref, back_ref, q_s, k_s, v_s, g_s, labels_s, dk_s, dv_s
):
    blocks = x_ref.shape[0] // message
    back = back_ref.shape[0] // blocks
    groups = blocks // LANES
    tile = SLOTS * LANES
    slots = blocks * SLOTS
    scale = LANES ** (-0.5)
    arrays = (q_s, k_s, v_s, g_s)
    rows_ref[...] = x_ref[...].astype(jnp.float32)
    key_at = SLOTS * (iota(tile, tile, 0) % LANES) + iota(tile, tile, 0) // LANES
    query_at = SLOTS * (iota(tile, tile, 1) % LANES) + iota(tile, tile, 1) // LANES
    causal = key_at <= query_at
    query_labels = [[None] * groups for _ in range(per_dest)]
    for group in range(groups):
        first_row = group * LANES * message
        for slot in range(SLOTS):
            at = (group * SLOTS + slot) * LANES
            for head in range(per_dest):
                for array, scratch in enumerate(arrays):
                    row = first_row + (head * len(arrays) + array) * SLOTS + slot
                    scratch[head * slots + at : head * slots + at + LANES, :] = rows_ref[
                        pl.ds(row, LANES, stride=message), :
                    ].astype(jnp.bfloat16)
            row = first_row + per_dest * len(arrays) * SLOTS + slot
            label = rows_ref[pl.ds(row, LANES, stride=message), :]
            turned = jnp.transpose(label)
            for head in range(per_dest):
                lane = head * (LANES // per_dest)
                labels_s[head * slots + at : head * slots + at + LANES, :] = jnp.broadcast_to(
                    label[:, lane : lane + 1], (LANES, LANES)
                )
                part = turned[lane : lane + 1, :]
                part = jnp.where(part > 0.5, part, -1.0)
                before = query_labels[head][group]
                query_labels[head][group] = part if slot == 0 else jnp.concatenate([before, part], axis=1)

    def tile_of(head, group):
        start = head * slots + group * tile
        return slice(start, start + tile)

    def score_stage(head, query_group):
        q_rows = q_s[tile_of(head, query_group), :]
        query_label = query_labels[head][query_group]
        scores = []
        highest = jnp.full((FOLD, tile), LOWEST_MAX, jnp.float32)
        for key_group in range(query_group + 1):
            raw = dot_last(k_s[tile_of(head, key_group), :], q_rows)
            start = head * slots + key_group * tile
            kept = []
            for at in range(0, tile, FOLD):
                key_label = labels_s[start + at : start + at + FOLD, :]
                allowed = jnp.concatenate([key_label, key_label], axis=1) == query_label
                if key_group == query_group:
                    allowed = allowed & causal[at : at + FOLD, :]
                kept.append(jnp.where(allowed, raw[at : at + FOLD, :], MASKED_SCORE))
                highest = jnp.maximum(highest, kept[-1])
            scores.append(kept)
        return scores, jnp.max(highest, axis=0, keepdims=True)

    def gradient_stage(head, query_group, scores, row_max):
        own = tile_of(head, query_group)
        q_rows, g_rows = q_s[own, :], g_s[own, :]
        total = jnp.zeros((FOLD, tile), jnp.float32)
        weighted = jnp.zeros((FOLD, tile), jnp.float32)
        weights, grads = [], []
        for key_group in range(query_group + 1):
            prob_grad = dot_last(v_s[tile_of(head, key_group), :], g_rows)
            kept, split = [], []
            for index, at in enumerate(range(0, tile, FOLD)):
                weight = jnp.exp2((scores[key_group][index] - row_max) * (scale * LOG2_E))
                grad = prob_grad[at : at + FOLD, :]
                total = total + weight
                weighted = weighted + weight * grad
                kept.append(weight)
                split.append(grad)
            weights.append(kept)
            grads.append(split)
        inverse = 1.0 / jnp.maximum(jnp.sum(total, axis=0, keepdims=True), 1.0)
        delta = jnp.sum(weighted, axis=0, keepdims=True) * inverse
        query_grad = jnp.zeros((LANES, tile), jnp.float32)
        for key_group in range(query_group + 1):
            keys = tile_of(head, key_group)
            probs, score_grads = [], []
            for index in range(0, tile // FOLD, 2):
                pair = []
                for part in (index, index + 1):
                    prob = weights[key_group][part] * inverse
                    pair.append((prob, prob * (grads[key_group][part] - delta)))
                probs.append(jnp.concatenate([pair[0][0], pair[1][0]], axis=0).astype(jnp.bfloat16))
                score_grads.append(jnp.concatenate([pair[0][1], pair[1][1]], axis=0).astype(jnp.bfloat16))
            prob = jnp.concatenate(probs, axis=0)
            score_grad = jnp.concatenate(score_grads, axis=0)
            value_part = dot(prob, g_rows)
            key_part = dot(score_grad, q_rows)
            if key_group == query_group:
                dv_s[keys, :] = value_part
                dk_s[keys, :] = key_part
            else:
                dv_s[keys, :] += value_part
                dk_s[keys, :] += key_part
            query_grad = query_grad + lax.dot_general(
                k_s[keys, :],
                score_grad,
                (((0,), (0,)), ((), ())),
                preferred_element_type=jnp.float32,
            )
        query_rows = jnp.transpose(query_grad) * scale
        for slot in range(SLOTS):
            row = query_group * LANES * back + head * 3 * SLOTS + slot
            back_ref[pl.ds(row, LANES, stride=back), :] = query_rows[slot * LANES : (slot + 1) * LANES, :]

    units = [(head, group) for group in range(groups) for head in range(per_dest)]
    ahead = score_stage(*units[0])
    for index, unit in enumerate(units):
        scores, row_max = ahead
        if index + 1 < len(units):
            ahead = score_stage(*units[index + 1])
        gradient_stage(*unit, scores, row_max)
    for head in range(per_dest):
        for array, grad, factor in ((1, dk_s, scale), (2, dv_s, 1.0)):
            for group in range(groups):
                for slot in range(SLOTS):
                    row = group * LANES * back + (head * 3 + array) * SLOTS + slot
                    at = head * slots + (group * SLOTS + slot) * LANES
                    back_ref[pl.ds(row, LANES, stride=back), :] = grad[at : at + LANES, :] * factor
    out_ref[...] = back_ref[...].astype(jnp.bfloat16)


def unplace_kernel(
    owners, spills, y_ref, select_ref, dq_hbm, dk_hbm, dv_hbm, rows_ref, dq_ref, dk_ref, dv_ref, sems
):
    tokens = dq_ref.shape[0]
    heads = select_ref.shape[0] // tokens
    per_dest = heads // spills
    width = per_dest * LANES
    outs = (dq_ref, dk_ref, dv_ref)
    back = per_dest * len(outs) * SLOTS
    rows_ref[...] = y_ref[...].astype(jnp.float32)
    copies = []
    for head in range(heads):
        dest, within = divmod(head, per_dest)
        stacked = []
        for array in range(len(outs)):
            slots = []
            for slot in range(SLOTS):
                row = dest * back + (within * len(outs) + array) * SLOTS + slot
                slots.append(rows_ref[pl.ds(row, owners, stride=spills * back), :])
            stacked.append(jnp.concatenate(slots, axis=0).astype(jnp.bfloat16))
        select = select_ref[head * tokens : (head + 1) * tokens, :]
        result = dot(select, jnp.concatenate(stacked, axis=1)).astype(jnp.bfloat16)
        for array, ref in enumerate(outs):
            ref[:, head * LANES : (head + 1) * LANES] = result[:, array * LANES : (array + 1) * LANES]
        if within == per_dest - 1:
            columns = slice(dest * width, (dest + 1) * width)
            for array, (source, target) in enumerate(zip(outs, (dq_hbm, dk_hbm, dv_hbm))):
                copies.append(
                    pltpu.make_async_copy(
                        source.at[:, columns], target.at[:, columns], sems.at[dest * len(outs) + array]
                    )
                )
                copies[-1].start()
    for copy in copies:
        copy.wait()


def local_ops(owners, spills, tokens, heads):
    devices = owners * spills
    per_dest = heads // spills
    message = per_dest * 4 * SLOTS + SLOTS
    back = per_dest * 3 * SLOTS
    slots = devices * SLOTS
    width = heads * LANES
    whole = pl.BlockSpec(memory_space=pltpu.VMEM)
    hbm = pl.BlockSpec(memory_space=pltpu.HBM)
    params = pltpu.CompilerParams(vmem_limit_bytes=48 * 1024 * 1024)
    token_rows = pltpu.VMEM((tokens, width), jnp.bfloat16)
    grad_shape = jax.ShapeDtypeStruct((tokens, width), jnp.bfloat16)
    place = pl.pallas_call(
        functools.partial(place_kernel, owners, spills),
        out_shape=(
            jax.ShapeDtypeStruct((devices * message, LANES), jnp.bfloat16),
            jax.ShapeDtypeStruct((heads * tokens, SLOTS * owners), jnp.bfloat16),
        ),
        in_specs=[hbm] * 5,
        out_specs=(whole, whole),
        scratch_shapes=[token_rows] * 4
        + [
            pltpu.VMEM((heads, tokens), jnp.int32),
            pltpu.VMEM((heads * SLOTS * owners, tokens), jnp.bfloat16),
            pltpu.VMEM((devices * message, LANES), jnp.float32),
            pltpu.SemaphoreType.DMA((4 * spills + 1,)),
        ],
        compiler_params=params,
        name="place",
    )
    attend = pl.pallas_call(
        functools.partial(attend_kernel, per_dest, message),
        out_shape=jax.ShapeDtypeStruct((devices * back, LANES), jnp.bfloat16),
        in_specs=[whole],
        out_specs=whole,
        scratch_shapes=[
            pltpu.VMEM((devices * message, LANES), jnp.float32),
            pltpu.VMEM((devices * back, LANES), jnp.float32),
            pltpu.VMEM((per_dest * slots, LANES), jnp.bfloat16),
            pltpu.VMEM((per_dest * slots, LANES), jnp.bfloat16),
            pltpu.VMEM((per_dest * slots, LANES), jnp.bfloat16),
            pltpu.VMEM((per_dest * slots, LANES), jnp.bfloat16),
            pltpu.VMEM((per_dest * slots, LANES), jnp.float32),
            pltpu.VMEM((per_dest * slots, LANES), jnp.float32),
            pltpu.VMEM((per_dest * slots, LANES), jnp.float32),
        ],
        compiler_params=params,
        name="attend",
    )
    unplace = pl.pallas_call(
        functools.partial(unplace_kernel, owners, spills),
        out_shape=(grad_shape, grad_shape, grad_shape),
        in_specs=[whole] * 2,
        out_specs=(hbm, hbm, hbm),
        scratch_shapes=[pltpu.VMEM((devices * back, LANES), jnp.float32)]
        + [token_rows] * 3
        + [pltpu.SemaphoreType.DMA((3 * spills,))],
        compiler_params=params,
        name="unplace",
    )
    return place, attend, unplace


def local(queries, keys, values, out_grad, cluster_ids):
    owners, spills = lax.axis_size("seq"), lax.axis_size("spill")
    devices = owners * spills
    place, attend, unplace = local_ops(owners, spills, *cluster_ids.shape)

    def exchange(rows):
        cut = rows.reshape(devices, -1, SLOTS, LANES)
        moved = lax.all_to_all(cut, AXES, split_axis=0, concat_axis=0, tiled=True)
        return moved.reshape(rows.shape)

    inputs = (queries, keys, values, out_grad, jnp.transpose(cluster_ids))
    rows, select = place(*(pltpu.with_memory_space_constraint(x, pltpu.HBM) for x in inputs))
    return unplace(exchange(attend(exchange(rows))), select)


def solution(mesh):
    rows = P(AXES, None)
    return jax.shard_map(
        local,
        mesh=mesh,
        in_specs=(rows, rows, rows, rows, rows),
        out_specs=(rows, rows, rows),
        check_vma=False,
    )
```

time: 148 us -> 147 us (level)
  no operation moved by 1% of the time
where the time goes in v3:
time: 147 us
  blocking collectives  134 us (91%)
  Pallas kernels  11.4 us (8%)
    all_to_all x2, blocking collectives, exchange(): moved = lax.all_to_all(cut, AXES, split_axis=0, concat_axis=0, tiled=True)  134 us
    pallas_call x2, Pallas kernels, local(): return unplace(exchange(attend(exchange(rows))), select)  7.93 us
    pallas_call x1, Pallas kernels, local(): place(*(pltpu.with_memory_space_constraint(x, pltpu.HBM) for x in inputs))  3.45 us

profile of v3, /device:TPU:1, one launch (start us, length us, event | category | flops | bytes accessed | tf_op | source)
XLA Modules:
  0.0 146.7 jit_solution(248118587873511944)
XLA Ops:
  0.6 3.4 %place.1 = (bf16[9216,128]{1,0:T(8,128)(2,1)S(1)}, bf16[1024,256]{1,0:T(8,128)(2,1)S(1)}) custom-call(bf16[128,1024]{1,0:T(8,128)(2,1)} %q_hbm.1, bf16[128,1024]{1,0:T(8,128)(2,1)} %k_hbm.1, bf16[128,1024]{1,0:T(8,128)(2,1)} %v_hbm.1, bf16[128,1024]{1,0:T(8,128)(2,1)} %g_hbm.1, s32[8,128]{1,0:T(8,128)} %bitcast.9), custom_call_target="tpu_custom_call" | custom-call | tf_op jit(solution)/shard_map/place/pallas_call | solution.py:362
  4.1 81.8 %all_to_all.10 = bf16[512,9,2,128]{3,2,1,0:T(2,128)(2,1)S(1)} all-to-all(bf16[512,9,2,128]{3,2,1,0:T(2,128)(2,1)S(1)} %bitcast.8), channel_id=1, replica_groups=mesh['seq'=128,'spill'=4] {'seq','spill'}, dimensions={0} | all-to-all | bytes 4718592 | tf_op jit(solution)/shard_map/all_to_all | solution.py:358
  85.8 5.9 %attend.1 = bf16[6144,128]{1,0:T(8,128)(2,1)S(1)} custom-call(bf16[9216,128]{1,0:T(8,128)(2,1)S(1)} %bitcast.5), custom_call_target="tpu_custom_call" | custom-call | tf_op jit(solution)/shard_map/attend/pallas_call | solution.py:363
  91.8 52.7 %all_to_all.11 = bf16[512,6,2,128]{3,2,1,0:T(2,128)(2,1)S(1)} all-to-all(bf16[512,6,2,128]{3,2,1,0:T(2,128)(2,1)S(1)} %bitcast.7), channel_id=1, replica_groups=mesh['seq'=128,'spill'=4] {'seq','spill'}, dimensions={0} | all-to-all | bytes 3145728 | tf_op jit(solution)/shard_map/all_to_all | solution.py:358
  144.5 2.0 %unplace.1 = (bf16[128,1024]{1,0:T(8,128)(2,1)}, bf16[128,1024]{1,0:T(8,128)(2,1)}, bf16[128,1024]{1,0:T(8,128)(2,1)}) custom-call(bf16[6144,128]{1,0:T(8,128)(2,1)S(1)} %bitcast.6, bf16[1024,256]{1,0:T(8,128)(2,1)S(1)} %get-tuple-element.6.select_ref), custom_call_target="tpu_custom_call" | custom-call | tf_op jit(solution)/shard_map/unplace/pallas_call | solution.py:363

commit v4 on v3

--- a/solution.py
+++ b/solution.py
@@ -8,7 +8,9 @@
 from jax.experimental.pallas import tpu as pltpu
 from jax.sharding import PartitionSpec as P
 
-AXES = ("seq", "spill")
+RUN = 16
+AXES = ("outer", "inner", "spill")
+ROUTE = ("outer", "spill", "inner")
 LANES = 128
 SLOTS = 2
 FOLD = 8
@@ -35,6 +37,10 @@
     first = jnp.where(hot & (count < 0.5), 1.0, 0.0)
     second = jnp.where(hot & (count > 0.5), 1.0, 0.0)
     return first, second, jnp.concatenate([first, second], axis=axis).astype(jnp.bfloat16)
+
+
+def run_rows(spills, rows, run, spill, row):
+    return pl.ds((run * spills + spill) * RUN * rows + row, RUN, stride=rows)
 
 
 def place_kernel(
@@ -79,26 +85,30 @@
     after = jnp.where(iota(tokens, tokens, 1) < iota(tokens, tokens, 0), 1.0, 0.0).astype(jnp.bfloat16)
     half_lanes = iota(owners, LANES, 1) // (LANES // per_dest)
     ids_copy.wait()
-    id_columns = jnp.transpose(ids_ref[...].astype(jnp.float32)).astype(jnp.int32)
+    ids = ids_ref[...]
+    all_owners = ids % owners
+    all_labels = (ids // owners + 1).astype(jnp.float32)
+    owner_columns = jnp.transpose(all_owners.astype(jnp.float32)).astype(jnp.int32)
     for dest in range(spills):
         slot_labels = [jnp.zeros((owners, LANES), jnp.float32)] * SLOTS
         for within in range(per_dest):
             head = dest * per_dest + within
-            ids = jnp.broadcast_to(ids_ref[head : head + 1, :], (owners, tokens))
-            hot = ids % owners == iota(owners, tokens, 0)
+            hot = all_owners[head : head + 1, :] == iota(owners, tokens, 0)
             count = dot(jnp.where(hot, 1.0, 0.0).astype(jnp.bfloat16), before)
             first, second, select = one_hot_pair(hot, count, 0)
             select_ref[head * SLOTS * owners : (head + 1) * SLOTS * owners, :] = select
-            label = (ids // owners + 1).astype(jnp.float32)
+            label = all_labels[head : head + 1, :]
             for slot, mask in enumerate((first, second)):
                 slot_label = jnp.sum(mask * label, axis=1, keepdims=True)
                 slot_labels[slot] = jnp.where(half_lanes == within, slot_label, slot_labels[slot])
-            hot = id_columns[:, head : head + 1] % owners == iota(tokens, owners, 1)
+            hot = owner_columns[:, head : head + 1] == iota(tokens, owners, 1)
             count = dot(after, jnp.where(hot, 1.0, 0.0).astype(jnp.bfloat16))
             return_ref[head * tokens : (head + 1) * tokens, :] = one_hot_pair(hot, count, 1)[2]
         for slot in range(SLOTS):
-            row = dest * message + data_rows + slot
-            rows_ref[pl.ds(row, owners, stride=spills * message), :] = slot_labels[slot]
+            for run in range(owners // RUN):
+                rows_ref[run_rows(spills, message, run, dest, data_rows + slot), :] = slot_labels[slot][
+                    run * RUN : (run + 1) * RUN, :
+                ]
     for head in range(heads):
         dest, within = divmod(head, per_dest)
         if within == 0:
@@ -111,15 +121,17 @@
         )
         for array in range(len(arrays)):
             for slot in range(SLOTS):
-                row = dest * message + (within * len(arrays) + array) * SLOTS + slot
-                rows_ref[pl.ds(row, owners, stride=spills * message), :] = placed[
-                    slot * owners : (slot + 1) * owners, array * LANES : (array + 1) * LANES
-                ]
+                row = (within * len(arrays) + array) * SLOTS + slot
+                for run in range(owners // RUN):
+                    at = slot * owners + run * RUN
+                    rows_ref[run_rows(spills, message, run, dest, row), :] = placed[
+                        at : at + RUN, array * LANES : (array + 1) * LANES
+                    ]
     out_ref[...] = rows_ref[...].astype(jnp.bfloat16)
 
 
 def attend_kernel(
-    per_dest, message, x_ref, out_ref, rows_ref, back_ref, q_s, k_s, v_s, g_s, labels_s, dk_s, dv_s
+    spills, per_dest, message, x_ref, out_ref, rows_ref, back_ref, q_s, k_s, v_s, g_s, labels_s, dk_s, dv_s
 ):
     blocks = x_ref.shape[0] // message
     back = back_ref.shape[0] // blocks
@@ -129,9 +141,15 @@
     scale = LANES ** (-0.5)
     arrays = (q_s, k_s, v_s, g_s)
     rows_ref[...] = x_ref[...].astype(jnp.float32)
-    key_at = SLOTS * (iota(tile, tile, 0) % LANES) + iota(tile, tile, 0) // LANES
-    query_at = SLOTS * (iota(tile, tile, 1) % LANES) + iota(tile, tile, 1) // LANES
-    causal = key_at <= query_at
+
+    def position(rows, columns, axis):
+        index = iota(rows, columns, axis)
+        block = index % LANES
+        run, spill = block // (spills * RUN), block // RUN % spills
+        return SLOTS * (spills * (run * RUN + block % RUN) + spill) + index // LANES
+
+    key_position = position(tile, LANES, 0)
+    query_position = position(FOLD, tile, 1)
     query_labels = [[None] * groups for _ in range(per_dest)]
     for group in range(groups):
         first_row = group * LANES * message
@@ -173,7 +191,8 @@
                 key_label = labels_s[start + at : start + at + FOLD, :]
                 allowed = jnp.concatenate([key_label, key_label], axis=1) == query_label
                 if key_group == query_group:
-                    allowed = allowed & causal[at : at + FOLD, :]
+                    key_at = key_position[at : at + FOLD, :]
+                    allowed = allowed & (jnp.concatenate([key_at, key_at], axis=1) <= query_position)
                 kept.append(jnp.where(allowed, raw[at : at + FOLD, :], MASKED_SCORE))
                 highest = jnp.maximum(highest, kept[-1])
             scores.append(kept)
@@ -265,8 +284,9 @@
         for array in range(len(outs)):
             slots = []
             for slot in range(SLOTS):
-                row = dest * back + (within * len(outs) + array) * SLOTS + slot
-                slots.append(rows_ref[pl.ds(row, owners, stride=spills * back), :])
+                row = (within * len(outs) + array) * SLOTS + slot
+                for run in range(owners // RUN):
+                    slots.append(rows_ref[run_rows(spills, back, run, dest, row), :])
             stacked.append(jnp.concatenate(slots, axis=0).astype(jnp.bfloat16))
         select = select_ref[head * tokens : (head + 1) * tokens, :]
         result = dot(select, jnp.concatenate(stacked, axis=1)).astype(jnp.bfloat16)
@@ -316,7 +336,7 @@
         name="place",
     )
     attend = pl.pallas_call(
-        functools.partial(attend_kernel, per_dest, message),
+        functools.partial(attend_kernel, spills, per_dest, message),
         out_shape=jax.ShapeDtypeStruct((devices * back, LANES), jnp.bfloat16),
         in_specs=[whole],
         out_specs=whole,
@@ -349,13 +369,13 @@
 
 
 def local(queries, keys, values, out_grad, cluster_ids):
-    owners, spills = lax.axis_size("seq"), lax.axis_size("spill")
+    owners, spills = lax.axis_size("outer") * RUN, lax.axis_size("spill")
     devices = owners * spills
     place, attend, unplace = local_ops(owners, spills, *cluster_ids.shape)
 
     def exchange(rows):
         cut = rows.reshape(devices, -1, SLOTS, LANES)
-        moved = lax.all_to_all(cut, AXES, split_axis=0, concat_axis=0, tiled=True)
+        moved = lax.all_to_all(cut, ROUTE, split_axis=0, concat_axis=0, tiled=True)
         return moved.reshape(rows.shape)
 
     inputs = (queries, keys, values, out_grad, jnp.transpose(cluster_ids))
@@ -364,6 +384,8 @@
 
 
 def solution(mesh):
+    cut = mesh.devices.reshape(-1, RUN, mesh.shape["spill"])
+    mesh = jax.sharding.Mesh(cut, AXES)
     rows = P(AXES, None)
     return jax.shard_map(
         local,

time: 147 us -> 148 us (level)
  blocking collectives: 134 us -> 137 us
    all_to_all x2, blocking collectives: 134 us -> 137 us  [exchange(): moved = lax.all_to_all(cut, ROUTE, split_axis=0, concat_axis=0, tiled=True)]
where the time goes in v4:
time: 148 us
  blocking collectives  137 us (93%)
  Pallas kernels  10.5 us (7%)
    all_to_all x2, blocking collectives, exchange(): moved = lax.all_to_all(cut, ROUTE, split_axis=0, concat_axis=0, tiled=True)  137 us
    pallas_call x2, Pallas kernels, local(): return unplace(exchange(attend(exchange(rows))), select)  7.32 us
    pallas_call x1, Pallas kernels, local(): place(*(pltpu.with_memory_space_constraint(x, pltpu.HBM) for x in inputs))  3.21 us

profile of v4, /device:TPU:1, one launch (start us, length us, event | category | flops | bytes accessed | tf_op | source)
XLA Modules:
  0.0 148.1 jit_solution(1069406882222782907)
XLA Ops:
  0.6 3.2 %place.1 = (bf16[9216,128]{1,0:T(8,128)(2,1)S(1)}, bf16[1024,256]{1,0:T(8,128)(2,1)S(1)}) custom-call(bf16[128,1024]{1,0:T(8,128)(2,1)} %q_hbm.1, bf16[128,1024]{1,0:T(8,128)(2,1)} %k_hbm.1, bf16[128,1024]{1,0:T(8,128)(2,1)} %v_hbm.1, bf16[128,1024]{1,0:T(8,128)(2,1)} %g_hbm.1, s32[8,128]{1,0:T(8,128)} %bitcast.9), custom_call_target="tpu_custom_call" | custom-call | tf_op jit(solution)/shard_map/place/pallas_call | solution.py:382
  3.8 82.4 %all_to_all.10 = bf16[512,9,2,128]{3,2,1,0:T(2,128)(2,1)S(1)} all-to-all(bf16[512,9,2,128]{3,2,1,0:T(2,128)(2,1)S(1)} %bitcast.8), channel_id=1, replica_groups=mesh['outer'=8,'inner'=16,'spill'=4] {'outer','spill','inner'}, dimensions={0} | all-to-all | bytes 4718592 | tf_op jit(solution)/shard_map/all_to_all | solution.py:378
  86.3 6.0 %attend.1 = bf16[6144,128]{1,0:T(8,128)(2,1)S(1)} custom-call(bf16[9216,128]{1,0:T(8,128)(2,1)S(1)} %bitcast.5), custom_call_target="tpu_custom_call" | custom-call | tf_op jit(solution)/shard_map/attend/pallas_call | solution.py:383
  92.3 54.3 %all_to_all.11 = bf16[512,6,2,128]{3,2,1,0:T(2,128)(2,1)S(1)} all-to-all(bf16[512,6,2,128]{3,2,1,0:T(2,128)(2,1)S(1)} %bitcast.7), channel_id=1, replica_groups=mesh['outer'=8,'inner'=16,'spill'=4] {'outer','spill','inner'}, dimensions={0} | all-to-all | bytes 3145728 | tf_op jit(solution)/shard_map/all_to_all | solution.py:378
  146.6 1.4 unplace.1

commit v5 on v3

--- a/solution.py
+++ b/solution.py
@@ -74,31 +74,34 @@
             copies[-1].start()
     data_rows = per_dest * len(arrays) * SLOTS
     message = data_rows + SLOTS
+    pitch = spills * message + 1
     token_before = iota(tokens, tokens, 0) < iota(tokens, tokens, 1)
     before = jnp.where(token_before, 1.0, 0.0).astype(jnp.bfloat16)
     after = jnp.where(iota(tokens, tokens, 1) < iota(tokens, tokens, 0), 1.0, 0.0).astype(jnp.bfloat16)
     half_lanes = iota(owners, LANES, 1) // (LANES // per_dest)
     ids_copy.wait()
-    id_columns = jnp.transpose(ids_ref[...].astype(jnp.float32)).astype(jnp.int32)
+    ids = ids_ref[...]
+    all_owners = ids % owners
+    all_labels = (ids // owners + 1).astype(jnp.float32)
+    owner_columns = jnp.transpose(all_owners.astype(jnp.float32)).astype(jnp.int32)
     for dest in range(spills):
         slot_labels = [jnp.zeros((owners, LANES), jnp.float32)] * SLOTS
         for within in range(per_dest):
             head = dest * per_dest + within
-            ids = jnp.broadcast_to(ids_ref[head : head + 1, :], (owners, tokens))
-            hot = ids % owners == iota(owners, tokens, 0)
+            hot = all_owners[head : head + 1, :] == iota(owners, tokens, 0)
             count = dot(jnp.where(hot, 1.0, 0.0).astype(jnp.bfloat16), before)
             first, second, select = one_hot_pair(hot, count, 0)
             select_ref[head * SLOTS * owners : (head + 1) * SLOTS * owners, :] = select
-            label = (ids // owners + 1).astype(jnp.float32)
+            label = all_labels[head : head + 1, :]
             for slot, mask in enumerate((first, second)):
                 slot_label = jnp.sum(mask * label, axis=1, keepdims=True)
                 slot_labels[slot] = jnp.where(half_lanes == within, slot_label, slot_labels[slot])
-            hot = id_columns[:, head : head + 1] % owners == iota(tokens, owners, 1)
+            hot = owner_columns[:, head : head + 1] == iota(tokens, owners, 1)
             count = dot(after, jnp.where(hot, 1.0, 0.0).astype(jnp.bfloat16))
             return_ref[head * tokens : (head + 1) * tokens, :] = one_hot_pair(hot, count, 1)[2]
         for slot in range(SLOTS):
             row = dest * message + data_rows + slot
-            rows_ref[pl.ds(row, owners, stride=spills * message), :] = slot_labels[slot]
+            rows_ref[pl.ds(row, owners, stride=pitch), :] = slot_labels[slot]
     for head in range(heads):
         dest, within = divmod(head, per_dest)
         if within == 0:
@@ -112,23 +115,27 @@
         for array in range(len(arrays)):
             for slot in range(SLOTS):
                 row = dest * message + (within * len(arrays) + array) * SLOTS + slot
-                rows_ref[pl.ds(row, owners, stride=spills * message), :] = placed[
+                rows_ref[pl.ds(row, owners, stride=pitch), :] = placed[
                     slot * owners : (slot + 1) * owners, array * LANES : (array + 1) * LANES
                 ]
-    out_ref[...] = rows_ref[...].astype(jnp.bfloat16)
+    for owner in range(0, owners, 2):
+        pair = [rows_ref[at * pitch : (at + 1) * pitch - 1, :] for at in (owner, owner + 1)]
+        out_ref[owner * (pitch - 1) : (owner + 2) * (pitch - 1), :] = jnp.concatenate(pair, axis=0).astype(
+            jnp.bfloat16
+        )
 
 
 def attend_kernel(
     per_dest, message, x_ref, out_ref, rows_ref, back_ref, q_s, k_s, v_s, g_s, labels_s, dk_s, dv_s
 ):
     blocks = x_ref.shape[0] // message
-    back = back_ref.shape[0] // blocks
+    back = out_ref.shape[0] // blocks
     groups = blocks // LANES
     tile = SLOTS * LANES
     slots = blocks * SLOTS
     scale = LANES ** (-0.5)
     arrays = (q_s, k_s, v_s, g_s)
-    rows_ref[...] = x_ref[...].astype(jnp.float32)
+    rows_ref[: x_ref.shape[0], :] = x_ref[...].astype(jnp.float32)
     key_at = SLOTS * (iota(tile, tile, 0) % LANES) + iota(tile, tile, 0) // LANES
     query_at = SLOTS * (iota(tile, tile, 1) % LANES) + iota(tile, tile, 1) // LANES
     causal = key_at <= query_at
@@ -245,7 +252,7 @@
                     row = group * LANES * back + (head * 3 + array) * SLOTS + slot
                     at = head * slots + (group * SLOTS + slot) * LANES
                     back_ref[pl.ds(row, LANES, stride=back), :] = grad[at : at + LANES, :] * factor
-    out_ref[...] = back_ref[...].astype(jnp.bfloat16)
+    out_ref[...] = back_ref[: out_ref.shape[0], :].astype(jnp.bfloat16)
 
 
 def unplace_kernel(
@@ -257,7 +264,11 @@
     width = per_dest * LANES
     outs = (dq_ref, dk_ref, dv_ref)
     back = per_dest * len(outs) * SLOTS
-    rows_ref[...] = y_ref[...].astype(jnp.float32)
+    pitch = spills * back + 1
+    for owner in range(owners):
+        rows_ref[owner * pitch : (owner + 1) * pitch - 1, :] = y_ref[
+            owner * (pitch - 1) : (owner + 1) * (pitch - 1), :
+        ].astype(jnp.float32)
     copies = []
     for head in range(heads):
         dest, within = divmod(head, per_dest)
@@ -266,7 +277,7 @@
             slots = []
             for slot in range(SLOTS):
                 row = dest * back + (within * len(outs) + array) * SLOTS + slot
-                slots.append(rows_ref[pl.ds(row, owners, stride=spills * back), :])
+                slots.append(rows_ref[pl.ds(row, owners, stride=pitch), :])
             stacked.append(jnp.concatenate(slots, axis=0).astype(jnp.bfloat16))
         select = select_ref[head * tokens : (head + 1) * tokens, :]
         result = dot(select, jnp.concatenate(stacked, axis=1)).astype(jnp.bfloat16)
@@ -283,6 +294,10 @@
                 copies[-1].start()
     for copy in copies:
         copy.wait()
+
+
+def strided_rows(count, pitch):
+    return pltpu.VMEM((-(-(count + 1) * pitch // FOLD) * FOLD, LANES), jnp.float32)
 
 
 def local_ops(owners, spills, tokens, heads):
@@ -309,7 +324,7 @@
         + [
             pltpu.VMEM((heads, tokens), jnp.int32),
             pltpu.VMEM((heads * SLOTS * owners, tokens), jnp.bfloat16),
-            pltpu.VMEM((devices * message, LANES), jnp.float32),
+            strided_rows(owners, spills * message + 1),
             pltpu.SemaphoreType.DMA((4 * spills + 1,)),
         ],
         compiler_params=params,
@@ -321,8 +336,8 @@
         in_specs=[whole],
         out_specs=whole,
         scratch_shapes=[
-            pltpu.VMEM((devices * message, LANES), jnp.float32),
-            pltpu.VMEM((devices * back, LANES), jnp.float32),
+            strided_rows(devices, message),
+            strided_rows(devices, back),
             pltpu.VMEM((per_dest * slots, LANES), jnp.bfloat16),
             pltpu.VMEM((per_dest * slots, LANES), jnp.bfloat16),
             pltpu.VMEM((per_dest * slots, LANES), jnp.bfloat16),
@@ -339,7 +354,7 @@
         out_shape=(grad_shape, grad_shape, grad_shape),
         in_specs=[whole] * 2,
         out_specs=(hbm, hbm, hbm),
-        scratch_shapes=[pltpu.VMEM((devices * back, LANES), jnp.float32)]
+        scratch_shapes=[strided_rows(owners, spills * back + 1)]
         + [token_rows] * 3
         + [pltpu.SemaphoreType.DMA((3 * spills,))],
         compiler_params=params,

time: 147 us -> 146 us (level)
  no operation moved by 1% of the time
where the time goes in v5:
time: 146 us
  blocking collectives  135 us (92%)
  Pallas kernels  10.4 us (7%)
    all_to_all x2, blocking collectives, exchange(): moved = lax.all_to_all(cut, AXES, split_axis=0, concat_axis=0, tiled=True)  135 us
    pallas_call x2, Pallas kernels, local(): return unplace(exchange(attend(exchange(rows))), select)  7.26 us
    pallas_call x1, Pallas kernels, local(): place(*(pltpu.with_memory_space_constraint(x, pltpu.HBM) for x in inputs))  3.19 us

profile of v5, /device:TPU:1, one launch (start us, length us, event | category | flops | bytes accessed | tf_op | source)
XLA Modules:
  0.0 145.8 jit_solution(16242750188657123067)
XLA Ops:
  0.6 3.2 %place.1 = (bf16[9216,128]{1,0:T(8,128)(2,1)S(1)}, bf16[1024,256]{1,0:T(8,128)(2,1)S(1)}) custom-call(bf16[128,1024]{1,0:T(8,128)(2,1)} %q_hbm.1, bf16[128,1024]{1,0:T(8,128)(2,1)} %k_hbm.1, bf16[128,1024]{1,0:T(8,128)(2,1)} %v_hbm.1, bf16[128,1024]{1,0:T(8,128)(2,1)} %g_hbm.1, s32[8,128]{1,0:T(8,128)} %bitcast.9), custom_call_target="tpu_custom_call" | custom-call | tf_op jit(solution)/shard_map/place/pallas_call | solution.py:377
  3.8 81.8 %all_to_all.10 = bf16[512,9,2,128]{3,2,1,0:T(2,128)(2,1)S(1)} all-to-all(bf16[512,9,2,128]{3,2,1,0:T(2,128)(2,1)S(1)} %bitcast.8), channel_id=1, replica_groups=mesh['seq'=128,'spill'=4] {'seq','spill'}, dimensions={0} | all-to-all | bytes 4718592 | tf_op jit(solution)/shard_map/all_to_all | solution.py:373
  85.6 5.9 %attend.1 = bf16[6144,128]{1,0:T(8,128)(2,1)S(1)} custom-call(bf16[9216,128]{1,0:T(8,128)(2,1)S(1)} %bitcast.5), custom_call_target="tpu_custom_call" | custom-call | tf_op jit(solution)/shard_map/attend/pallas_call | solution.py:378
  91.5 52.7 %all_to_all.11 = bf16[512,6,2,128]{3,2,1,0:T(2,128)(2,1)S(1)} all-to-all(bf16[512,6,2,128]{3,2,1,0:T(2,128)(2,1)S(1)} %bitcast.7), channel_id=1, replica_groups=mesh['seq'=128,'spill'=4] {'seq','spill'}, dimensions={0} | all-to-all | bytes 3145728 | tf_op jit(solution)/shard_map/all_to_all | solution.py:373
  144.2 1.4 unplace.1

commit v6 on v5

--- a/solution.py
+++ b/solution.py
@@ -58,20 +58,13 @@
 ):
     heads, tokens = ids_ref.shape
     per_dest = heads // spills
-    width = per_dest * LANES
     arrays = (q_ref, k_ref, v_ref, g_ref)
-    ids_copy = pltpu.make_async_copy(ids_hbm, ids_ref, sems.at[len(arrays) * spills])
+    ids_copy = pltpu.make_async_copy(ids_hbm, ids_ref, sems.at[len(arrays)])
     ids_copy.start()
     copies = []
-    for dest in range(spills):
-        columns = slice(dest * width, (dest + 1) * width)
-        for array, (source, target) in enumerate(zip((q_hbm, k_hbm, v_hbm, g_hbm), arrays)):
-            copies.append(
-                pltpu.make_async_copy(
-                    source.at[:, columns], target.at[:, columns], sems.at[dest * len(arrays) + array]
-                )
-            )
-            copies[-1].start()
+    for array, (source, target) in enumerate(zip((q_hbm, k_hbm, v_hbm, g_hbm), arrays)):
+        copies.append(pltpu.make_async_copy(source, target, sems.at[array]))
+        copies[-1].start()
     data_rows = per_dest * len(arrays) * SLOTS
     message = data_rows + SLOTS
     pitch = spills * message + 1
@@ -84,7 +77,8 @@
     all_owners = ids % owners
     all_labels = (ids // owners + 1).astype(jnp.float32)
     owner_columns = jnp.transpose(all_owners.astype(jnp.float32)).astype(jnp.int32)
-    for dest in range(spills):
+
+    def choose(dest):
         slot_labels = [jnp.zeros((owners, LANES), jnp.float32)] * SLOTS
         for within in range(per_dest):
             head = dest * per_dest + within
@@ -96,28 +90,35 @@
             for slot, mask in enumerate((first, second)):
                 slot_label = jnp.sum(mask * label, axis=1, keepdims=True)
                 slot_labels[slot] = jnp.where(half_lanes == within, slot_label, slot_labels[slot])
+        for slot in range(SLOTS):
+            row = dest * message + data_rows + slot
+            rows_ref[pl.ds(row, owners, stride=pitch), :] = slot_labels[slot]
+
+    def choose_return(dest):
+        for head in range(dest * per_dest, (dest + 1) * per_dest):
             hot = owner_columns[:, head : head + 1] == iota(tokens, owners, 1)
             count = dot(after, jnp.where(hot, 1.0, 0.0).astype(jnp.bfloat16))
             return_ref[head * tokens : (head + 1) * tokens, :] = one_hot_pair(hot, count, 1)[2]
-        for slot in range(SLOTS):
-            row = dest * message + data_rows + slot
-            rows_ref[pl.ds(row, owners, stride=pitch), :] = slot_labels[slot]
-    for head in range(heads):
-        dest, within = divmod(head, per_dest)
-        if within == 0:
-            for copy in copies[dest * len(arrays) : (dest + 1) * len(arrays)]:
-                copy.wait()
-        columns = slice(head * LANES, (head + 1) * LANES)
-        placed = dot(
-            select_ref[head * SLOTS * owners : (head + 1) * SLOTS * owners, :],
-            jnp.concatenate([ref[:, columns] for ref in arrays], axis=1),
-        )
-        for array in range(len(arrays)):
-            for slot in range(SLOTS):
-                row = dest * message + (within * len(arrays) + array) * SLOTS + slot
-                rows_ref[pl.ds(row, owners, stride=pitch), :] = placed[
-                    slot * owners : (slot + 1) * owners, array * LANES : (array + 1) * LANES
-                ]
+
+    for dest in range(spills):
+        choose(dest)
+    for copy in copies:
+        copy.wait()
+    for dest in range(spills):
+        for within in range(per_dest):
+            head = dest * per_dest + within
+            columns = slice(head * LANES, (head + 1) * LANES)
+            placed = dot(
+                select_ref[head * SLOTS * owners : (head + 1) * SLOTS * owners, :],
+                jnp.concatenate([ref[:, columns] for ref in arrays], axis=1),
+            )
+            for array in range(len(arrays)):
+                for slot in range(SLOTS):
+                    row = dest * message + (within * len(arrays) + array) * SLOTS + slot
+                    rows_ref[pl.ds(row, owners, stride=pitch), :] = placed[
+                        slot * owners : (slot + 1) * owners, array * LANES : (array + 1) * LANES
+                    ]
+        choose_return(dest)
     for owner in range(0, owners, 2):
         pair = [rows_ref[at * pitch : (at + 1) * pitch - 1, :] for at in (owner, owner + 1)]
         out_ref[owner * (pitch - 1) : (owner + 2) * (pitch - 1), :] = jnp.concatenate(pair, axis=0).astype(
@@ -325,7 +326,7 @@
             pltpu.VMEM((heads, tokens), jnp.int32),
             pltpu.VMEM((heads * SLOTS * owners, tokens), jnp.bfloat16),
             strided_rows(owners, spills * message + 1),
-            pltpu.SemaphoreType.DMA((4 * spills + 1,)),
+            pltpu.SemaphoreType.DMA((5,)),
         ],
         compiler_params=params,
         name="place",

time: 146 us -> 145 us (level)
  no operation moved by 1% of the time
where the time goes in v6:
time: 145 us
  blocking collectives  134 us (92%)
  Pallas kernels  9.59 us (7%)
    all_to_all x2, blocking collectives, exchange(): moved = lax.all_to_all(cut, AXES, split_axis=0, concat_axis=0, tiled=True)  134 us
    pallas_call x2, Pallas kernels, local(): return unplace(exchange(attend(exchange(rows))), select)  7.26 us

profile of v6, /device:TPU:1, one launch (start us, length us, event | category | flops | bytes accessed | tf_op | source)
XLA Modules:
  0.0 144.9 jit_solution(15920606761563722492)
XLA Ops:
  0.6 2.3 %place.1 = (bf16[9216,128]{1,0:T(8,128)(2,1)S(1)}, bf16[1024,256]{1,0:T(8,128)(2,1)S(1)}) custom-call(bf16[128,1024]{1,0:T(8,128)(2,1)} %q_hbm.1, bf16[128,1024]{1,0:T(8,128)(2,1)} %k_hbm.1, bf16[128,1024]{1,0:T(8,128)(2,1)} %v_hbm.1, bf16[128,1024]{1,0:T(8,128)(2,1)} %g_hbm.1, s32[8,128]{1,0:T(8,128)} %bitcast.9), custom_call_target="tpu_custom_call" | custom-call | tf_op jit(solution)/shard_map/place/pallas_call | solution.py:378
  3.0 81.7 %all_to_all.10 = bf16[512,9,2,128]{3,2,1,0:T(2,128)(2,1)S(1)} all-to-all(bf16[512,9,2,128]{3,2,1,0:T(2,128)(2,1)S(1)} %bitcast.8), channel_id=1, replica_groups=mesh['seq'=128,'spill'=4] {'seq','spill'}, dimensions={0} | all-to-all | bytes 4718592 | tf_op jit(solution)/shard_map/all_to_all | solution.py:374
  84.7 5.9 %attend.1 = bf16[6144,128]{1,0:T(8,128)(2,1)S(1)} custom-call(bf16[9216,128]{1,0:T(8,128)(2,1)S(1)} %bitcast.5), custom_call_target="tpu_custom_call" | custom-call | tf_op jit(solution)/shard_map/attend/pallas_call | solution.py:379
  90.6 52.7 %all_to_all.11 = bf16[512,6,2,128]{3,2,1,0:T(2,128)(2,1)S(1)} all-to-all(bf16[512,6,2,128]{3,2,1,0:T(2,128)(2,1)S(1)} %bitcast.7), channel_id=1, replica_groups=mesh['seq'=128,'spill'=4] {'seq','spill'}, dimensions={0} | all-to-all | bytes 3145728 | tf_op jit(solution)/shard_map/all_to_all | solution.py:374
  143.4 1.4 unplace.1
